TPU v7x, 32 devices: a whole 2x2x4 slice. The times are simulated.
32 devices in a mesh: section: 2 (over y), dp: 4 (over x, core), tensor: 4 (over z).
Axes of the slice: x: 2, y: 2, z: 4, core: 2. Of those that a mesh axis runs over, the one named last changes fastest.
Arguments:
- tokens: bfloat16 [4, 5, 256, 1024], P('dp', None, 'tensor'), may hold values from -6 to 6
- cotangent: float32 [4, 5, 256, 1024], P('dp', None, 'tensor'), may hold values from -6 to 6
- norm_gain: float32 [2, 1024], P('section'), may hold values from 0.5 to 1.5
- gate_weight: bfloat16 [2, 1024, 2048], P('section', 'dp', 'tensor'), may hold values from -0.1875 to 0.1875
- inner_weight: bfloat16 [2, 1024, 2048], P('section', 'dp', 'tensor'), may hold values from -0.1875 to 0.1875
- state_weight: bfloat16 [2, 1024, 256], P('section', 'dp'), may hold values from -0.1875 to 0.1875
- step_weight: bfloat16 [2, 1024, 32], P('section', 'dp', 'tensor'), may hold values from -0.25 to 0.25
- conv_inner: float32 [2, 5, 2048], P('section', None, 'tensor'), may hold values from -3 to 3
- conv_state: float32 [2, 5, 256], P('section'), may hold values from -3 to 3
- head_params: float32 [2, 3, 32], P('section', None, 'tensor'), may hold values from -7 to 1.4, as said below
- gate_gain: float32 [2, 2048], P('section'), may hold values from 0.5 to 1.5
- out_weight: bfloat16 [2, 2048, 1024], P('section', None, 'dp'), may hold values from -0.125 to 0.125
Outputs:
- output: float32 [2, 4, 5, 256, 1024], P('section', 'dp', None, 'tensor')
- input_grad: float32 [2, 4, 5, 256, 1024], P('section', 'dp', None, 'tensor')
- grad_norm_gain: float32 [2, 1024], P('section')
- grad_gate_weight: float32 [2, 1024, 2048], P('section', 'dp', 'tensor')
- grad_inner_weight: float32 [2, 1024, 2048], P('section', 'dp', 'tensor')
- grad_state_weight: float32 [2, 1024, 256], P('section', 'dp')
- grad_step_weight: float32 [2, 1024, 32], P('section', 'dp', 'tensor')
- grad_conv_inner: float32 [2, 5, 2048], P('section', None, 'tensor')
- grad_conv_state: float32 [2, 5, 256], P('section')
- grad_head_params: float32 [2, 3, 32], P('section', None, 'tensor')
- grad_gate_gain: float32 [2, 2048], P('section', 'tensor')
- grad_out_weight: float32 [2, 2048, 1024], P('section', 'tensor', 'dp')
Inputs may be any that keep to these rules, and one draw needn't show every extreme that they name: `head_params`: row 0 of each layer is added to the raw step sizes before softplus, row 1 is the logarithm of each head's decay rate, row 2 is each head's skip weight.
All inputs are finite; a program needn't handle non-finite values.
Results may differ from a plain program's by a relative error of at most 0.011.
Values may be sent and summed in bfloat16 or wider, within the bound.
A program may use at most 192 MiB of HBM per device.

v0:
```python
import jax
import jax.numpy as jnp
from jax import lax
from jax.sharding import PartitionSpec as P

D = 1024
HEADS = 32
HEADDIM = 64
STATE = 128
CONV = 4
INNER = 2048


EPSILON = 1e-05
FULL_PRECISION = lax.Precision.HIGHEST


def shifted(block, axis, distance):
    devices = range(lax.axis_size(axis))
    route = [(i - distance, i) for i in devices if i - distance in devices]
    return lax.ppermute(block, axis, route)


def causal_conv(padded, tap_rows):
    steps_out = padded.shape[0] - tap_rows.shape[0] + 2
    summed = tap_rows[-1] + jnp.zeros_like(padded[:steps_out])
    for offset in range(tap_rows.shape[0] - 1):
        summed = summed + tap_rows[offset] * padded[offset : offset + steps_out]
    return summed


def ssd_block(x_heads, b_state, c_state, step_size, decay_rate, skip_weight, carried):
    log_decay = step_size * decay_rate
    running = jnp.cumsum(log_decay, axis=0)
    length = running.shape[0]
    by_head = jnp.transpose(running, (1, 2, 0))
    spread = by_head[..., :, None] - by_head[..., None, :]
    causal_mask = lax.broadcasted_iota(jnp.int32, (length, length), 0) >= lax.broadcasted_iota(
        jnp.int32, (length, length), 1
    )
    kernel = jnp.where(causal_mask, jnp.exp(jnp.where(causal_mask, spread, 0.0)), 0.0)
    scores_cb = jnp.einsum("tbn,sbn->bts", c_state, b_state, precision=FULL_PRECISION)
    mixing = scores_cb[:, None] * kernel * jnp.transpose(step_size, (1, 2, 0))[:, :, None, :]
    inside = jnp.einsum("bhts,sbhp->tbhp", mixing, x_heads, precision=FULL_PRECISION)
    carried_out = (
        jnp.einsum("tbn,bhpn->tbhp", c_state, carried, precision=FULL_PRECISION)
        * jnp.exp(running)[..., None]
    )
    outputs = inside + carried_out + skip_weight[:, None] * x_heads
    last_sum = running[-1]
    weighting = jnp.exp(last_sum[None] - running) * step_size
    updated = jnp.exp(last_sum)[..., None, None] * carried + jnp.einsum(
        "sbh,sbhp,sbn->bhpn", weighting, x_heads, b_state, precision=FULL_PRECISION
    )
    return (outputs, updated)


def mixer_core(
    projected, step_raw, tail_inner, tail_state, carried, taps_inner, taps_state, head_rows
):
    width_loc = taps_inner.shape[1]
    heads_loc = head_rows.shape[1]
    joined_inner = jnp.concatenate([tail_inner, projected[..., width_loc : 2 * width_loc]], 0)
    joined_state = jnp.concatenate([tail_state, projected[..., 2 * width_loc :]], 0)
    inner_act = jax.nn.silu(causal_conv(joined_inner, taps_inner))
    state_act = jax.nn.silu(causal_conv(joined_state, taps_state))
    x_heads = inner_act.reshape(inner_act.shape[0], inner_act.shape[1], heads_loc, HEADDIM)
    step_size = jax.nn.softplus(step_raw + head_rows[0])
    head_out, updated = ssd_block(
        x_heads,
        state_act[..., :STATE],
        state_act[..., STATE:],
        step_size,
        -jnp.exp(head_rows[1]),
        head_rows[2],
        carried,
    )
    gate_out = head_out.reshape(inner_act.shape) * jax.nn.silu(projected[..., :width_loc])
    tail_rows = tail_inner.shape[0]
    return (gate_out, joined_inner[-tail_rows:], joined_state[-tail_rows:], updated)


def per_device(
    tokens,
    cotangent,
    norm_gain,
    gate_weight,
    inner_weight,
    state_weight,
    step_weight,
    conv_inner,
    conv_state,
    head_params,
    gate_gain,
    out_weight,
):
    tensor_rank = lax.axis_index("tensor")
    section_rank = lax.axis_index("section")
    first_section = section_rank == 0
    seq_count = tokens.shape[0]
    block_count = tokens.shape[1]
    part_rows = tokens.shape[2]
    width_loc = gate_weight.shape[2]
    heads_loc = step_weight.shape[2]
    row_start = tensor_rank * part_rows
    gain_rows = norm_gain[0]
    taps_inner = conv_inner[0]
    taps_state = conv_state[0]
    head_rows = head_params[0]
    gate_scale = lax.dynamic_slice_in_dim(gate_gain[0], tensor_rank * width_loc, width_loc, 0)
    out_local = lax.dynamic_slice_in_dim(out_weight[0], tensor_rank * width_loc, width_loc, 0)

    def fetch_weights():
        gate_full, inner_full, state_full, step_full, out_full = (
            lax.all_gather(gate_weight[0], "dp", axis=0, tiled=True),
            lax.all_gather(inner_weight[0], "dp", axis=0, tiled=True),
            lax.all_gather(state_weight[0], "dp", axis=0, tiled=True),
            lax.all_gather(step_weight[0], "dp", axis=0, tiled=True),
            lax.all_gather(out_local, "dp", axis=1, tiled=True),
        )
        return (jnp.concatenate([gate_full, inner_full, state_full], 1), step_full, out_full)

    def head_total(values):
        return lax.psum(values, "tensor")

    def place_local(values, length):
        canvas = jnp.zeros(values.shape[:-1] + (length,), jnp.float32)
        return lax.dynamic_update_slice_in_dim(
            canvas, values, tensor_rank * values.shape[-1], values.ndim - 1
        )

    source = jnp.transpose(tokens, (1, 2, 0, 3)).astype(jnp.float32)
    upstream = jnp.transpose(cotangent, (1, 2, 0, 3))
    zero_rows = jnp.zeros((part_rows, seq_count, D), jnp.float32)
    tail_inner = jnp.zeros((CONV - 1, seq_count, width_loc), jnp.float32)
    tail_state = jnp.zeros((CONV - 1, seq_count, 2 * STATE), jnp.float32)
    carried = jnp.zeros((seq_count, heads_loc, HEADDIM, STATE), jnp.float32)
    received = zero_rows
    kept_ticks = []
    layer_outs = []
    for tick_index in range(block_count + 1):
        proj_weights, step_weights, out_weights = fetch_weights()
        is_valid = (tick_index - section_rank >= 0) & (tick_index - section_rank < block_count)
        fresh_rows = source[tick_index] if tick_index < block_count else zero_rows
        hidden = jnp.where(first_section, fresh_rows, received)
        inv_rms = lax.rsqrt(jnp.mean(hidden * hidden, axis=2, keepdims=True) + EPSILON)
        normed = (hidden * inv_rms * gain_rows).astype(jnp.bfloat16)
        normed_full = lax.all_gather(normed, "tensor", axis=0, tiled=True)
        projected = jnp.einsum(
            "tbd,dc->tbc", normed_full, proj_weights, preferred_element_type=jnp.float32
        )
        step_raw = jnp.einsum(
            "tbd,dc->tbc", normed_full, step_weights, preferred_element_type=jnp.float32
        )
        mixer_out, pullback = jax.vjp(
            mixer_core,
            projected,
            step_raw,
            tail_inner,
            tail_state,
            carried,
            taps_inner,
            taps_state,
            head_rows,
        )
        gate_out, next_inner, next_state, next_carried = mixer_out
        inv_gate = lax.rsqrt(head_total(jnp.sum(gate_out * gate_out, axis=2)) / INNER + EPSILON)[
            ..., None
        ]
        normed_gate = (gate_out * inv_gate * gate_scale).astype(jnp.bfloat16)
        gate_rows = gate_out
        branch_out = lax.psum_scatter(
            jnp.einsum("tbc,cd->tbd", normed_gate, out_weights, preferred_element_type=jnp.float32),
            "tensor",
            scatter_dimension=0,
            tiled=True,
        )
        layer_out = hidden + branch_out
        tail_inner = jnp.where(is_valid, next_inner, tail_inner)
        tail_state = jnp.where(is_valid, next_state, tail_state)
        carried = jnp.where(is_valid, next_carried, carried)
        kept_ticks.append(
            (hidden, inv_rms, normed_full, pullback, normed_gate, inv_gate, gate_rows, is_valid)
        )
        layer_outs.append(layer_out)
        if tick_index < block_count:
            received = shifted(layer_out, "section", 1)
    back_inner = jnp.zeros_like(tail_inner)
    back_state = jnp.zeros_like(tail_state)
    back_carried = jnp.zeros_like(carried)
    gain_in_acc = jnp.zeros((D,), jnp.float32)
    gain_gate_acc = jnp.zeros(gate_scale.shape, jnp.float32)
    taps_inner_acc = jnp.zeros(taps_inner.shape, jnp.float32)
    taps_state_acc = jnp.zeros(taps_state.shape, jnp.float32)
    head_acc = jnp.zeros(head_rows.shape, jnp.float32)
    reduced = None
    received = zero_rows
    input_grads = []
    for back_turn in range(block_count + 1):
        hidden, inv_rms, normed_full, pullback, normed_gate, inv_gate, gate_rows, is_valid = (
            kept_ticks[block_count - back_turn]
        )
        proj_weights, step_weights, out_weights = fetch_weights()
        fresh_rows = upstream[block_count - 1 - back_turn] if back_turn < block_count else zero_rows
        grad_out = jnp.where(first_section, received, fresh_rows)
        grad_low = grad_out.astype(jnp.bfloat16)
        grad_full = lax.all_gather(grad_low, "tensor", axis=0, tiled=True)
        grad_norm_gate = jnp.einsum(
            "tbd,cd->tbc", grad_full, out_weights, preferred_element_type=jnp.float32
        )
        out_grad = jnp.einsum(
            "tbc,tbd->cd", normed_gate, grad_full, preferred_element_type=jnp.float32
        )
        gain_gate_grad = jnp.sum(grad_norm_gate * gate_rows * inv_gate, axis=(0, 1))
        inner_dot = head_total(jnp.sum(grad_norm_gate * gate_scale * gate_rows, axis=2))[..., None]
        grad_gate = (
            inv_gate * gate_scale * grad_norm_gate - gate_rows * inv_gate**3 * inner_dot / INNER
        )
        (
            grad_proj,
            grad_step,
            grad_tail_inner,
            grad_tail_state,
            grad_carried,
            grad_taps_inner,
            grad_taps_state,
            grad_head_rows,
        ) = pullback((grad_gate, back_inner, back_state, back_carried))
        state_total = lax.psum(grad_proj[..., 2 * width_loc :], "tensor")
        gate_inner_low = grad_proj[..., : 2 * width_loc].astype(jnp.bfloat16)
        state_low = state_total.astype(jnp.bfloat16)
        step_low = grad_step.astype(jnp.bfloat16)
        proj_grad = jnp.einsum(
            "tbd,tbc->dc",
            normed_full,
            jnp.concatenate([gate_inner_low, state_low], 2),
            preferred_element_type=jnp.float32,
        )
        step_grad = jnp.einsum(
            "tbd,tbc->dc", normed_full, step_low, preferred_element_type=jnp.float32
        )
        local_rows = jnp.einsum(
            "tbc,dc->tbd",
            gate_inner_low,
            proj_weights[:, : 2 * width_loc],
            preferred_element_type=jnp.float32,
        )
        grad_normed = lax.psum_scatter(
            local_rows
            + jnp.einsum("tbc,dc->tbd", step_low, step_weights, preferred_element_type=jnp.float32),
            "tensor",
            scatter_dimension=0,
            tiled=True,
        )
        grad_normed = grad_normed + jnp.einsum(
            "tbc,dc->tbd",
            lax.dynamic_slice_in_dim(state_low, row_start, part_rows, 0),
            proj_weights[:, 2 * width_loc :],
            preferred_element_type=jnp.float32,
        )
        gain_in_grad = jnp.sum(grad_normed * hidden * inv_rms, axis=(0, 1))
        inner_in = jnp.sum(grad_normed * gain_rows * hidden, axis=2, keepdims=True)
        grad_in = grad_out + inv_rms * gain_rows * grad_normed - hidden * inv_rms**3 * inner_in / D
        back_inner = jnp.where(is_valid, grad_tail_inner, back_inner)
        back_state = jnp.where(is_valid, grad_tail_state, back_state)
        back_carried = jnp.where(is_valid, grad_carried, back_carried)
        gain_in_acc = gain_in_acc + jnp.where(is_valid, gain_in_grad, 0.0)
        gain_gate_acc = gain_gate_acc + jnp.where(is_valid, gain_gate_grad, 0.0)
        taps_inner_acc = taps_inner_acc + jnp.where(is_valid, grad_taps_inner, 0.0)
        taps_state_acc = taps_state_acc + jnp.where(is_valid, grad_taps_state, 0.0)
        head_acc = head_acc + jnp.where(is_valid, grad_head_rows, 0.0)
        proj_grad = jnp.where(is_valid, proj_grad, 0.0)
        step_grad = jnp.where(is_valid, step_grad, 0.0)
        out_grad = jnp.where(is_valid, out_grad, 0.0)
        reduced_now = (
            lax.psum_scatter(proj_grad[:, :width_loc], "dp", scatter_dimension=0, tiled=True),
            lax.psum_scatter(
                proj_grad[:, width_loc : 2 * width_loc], "dp", scatter_dimension=0, tiled=True
            ),
            lax.psum_scatter(proj_grad[:, 2 * width_loc :], "dp", scatter_dimension=0, tiled=True),
            lax.psum_scatter(step_grad, "dp", scatter_dimension=0, tiled=True),
            lax.psum_scatter(out_grad, "dp", scatter_dimension=1, tiled=True),
        )
        reduced = (
            reduced_now
            if reduced is None
            else tuple((held_sum + extra_sum for held_sum, extra_sum in zip(reduced, reduced_now)))
        )
        input_grads.append(grad_in)
        if back_turn < block_count:
            received = shifted(grad_in, "section", -1)
    gain_gate_full = place_local(gain_gate_acc, INNER)
    small_sums = lax.psum(
        (
            gain_in_acc,
            place_local(taps_inner_acc, INNER),
            taps_state_acc,
            place_local(head_acc, HEADS),
            gain_gate_full,
        ),
        ("dp", "tensor"),
    )
    output = jnp.stack(
        [
            jnp.where(first_section, layer_outs[block_index], layer_outs[block_index + 1])
            for block_index in range(block_count)
        ]
    )
    input_grad = jnp.stack(
        [
            jnp.where(
                first_section,
                input_grads[block_count - block_index],
                input_grads[block_count - 1 - block_index],
            )
            for block_index in range(block_count)
        ]
    )
    return (
        jnp.transpose(output, (2, 0, 1, 3))[None],
        jnp.transpose(input_grad, (2, 0, 1, 3))[None],
        small_sums[0][None],
        reduced[0][None],
        reduced[1][None],
        reduced[2][None],
        reduced[3][None],
        lax.dynamic_slice_in_dim(small_sums[1], tensor_rank * width_loc, width_loc, 1)[None],
        small_sums[2][None],
        lax.dynamic_slice_in_dim(small_sums[3], tensor_rank * heads_loc, heads_loc, 1)[None],
        lax.dynamic_slice_in_dim(small_sums[4], tensor_rank * width_loc, width_loc, 0)[None],
        reduced[4][None],
    )


def solution(mesh):
    return jax.shard_map(
        per_device,
        mesh=mesh,
        in_specs=(
            P("dp", None, "tensor", None),
            P("dp", None, "tensor", None),
            P("section", None),
            P("section", "dp", "tensor"),
            P("section", "dp", "tensor"),
            P("section", "dp", None),
            P("section", "dp", "tensor"),
            P("section", None, "tensor"),
            P("section", None, None),
            P("section", None, "tensor"),
            P("section", None),
            P("section", None, "dp"),
        ),
        out_specs=(
            P("section", "dp", None, "tensor", None),
            P("section", "dp", None, "tensor", None),
            P("section", None),
            P("section", "dp", "tensor"),
            P("section", "dp", "tensor"),
            P("section", "dp", None),
            P("section", "dp", "tensor"),
            P("section", None, "tensor"),
            P("section", None, None),
            P("section", None, "tensor"),
            P("section", "tensor"),
            P("section", "tensor", "dp"),
        ),
        check_vma=False,
    )
```

profile of v0, /device:TPU:0, one launch (start us, length us, event | category | flops | bytes accessed | tf_op | source)
XLA Modules:
  0.0 1403.6 jit_solution(11290739010084219486)
XLA Ops:
  11.4 6.3 all-gather.3
  19.9 16.8 %all_gather.34 = bf16[256,1,1024]{2,0,1:T(8,128)(2,1)S(1)} all-gather(bf16[64,1,1024]{2,0,1:T(8,128)(2,1)S(1)} %multiply_convert_fusion.11), channel_id=1, replica_groups=mesh['section'=2,'dp'=4,'tensor'=4] {'tensor'}, dimensions={0}, use_global_device_ids=true | all-gather | bytes 655360 | tf_op jit(solution)/shard_map/all_gather | solution.py:148
  39.8 9.7 all-gather.2
  66.2 11.7 psum.161
  81.4 23.7 %reduce-scatter.18.cloned.1.call-done = f32[64,1,1024]{2,0,1:T(8,128)} async-done(((f32[256,1,1024]{2,0,1:T(8,128)}), f32[64,1,1024]{2,0,1:T(8,128)}) %reduce-scatter.18.cloned.1.call-update) | async-done | bytes 262160 | tf_op jit(solution)/shard_map/reduce_scatter | solution.py:172
  115.8 15.9 %all_gather.40 = bf16[256,1,1024]{2,0,1:T(8,128)(2,1)S(1)} all-gather(bf16[64,1,1024]{2,0,1:T(8,128)(2,1)S(1)} %multiply_convert_fusion.10), channel_id=1, replica_groups=mesh['section'=2,'dp'=4,'tensor'=4] {'tensor'}, dimensions={0}, use_global_device_ids=true | all-gather | bytes 655360 | tf_op jit(solution)/shard_map/all_gather | solution.py:148
  151.3 9.0 psum.162
  161.9 27.2 %reduce-scatter.20.cloned.1.call-done = f32[64,1,1024]{2,0,1:T(8,128)} async-done(((f32[256,1,1024]{2,0,1:T(8,128)}), f32[64,1,1024]{2,0,1:T(8,128)}) %reduce-scatter.20.cloned.1.call-update) | async-done | bytes 262160 | tf_op jit(solution)/shard_map/reduce_scatter | solution.py:172
  201.1 16.2 %all_gather.41 = bf16[256,1,1024]{2,0,1:T(8,128)(2,1)S(1)} all-gather(bf16[64,1,1024]{2,0,1:T(8,128)(2,1)S(1)} %multiply_convert_fusion.9), channel_id=1, replica_groups=mesh['section'=2,'dp'=4,'tensor'=4] {'tensor'}, dimensions={0}, use_global_device_ids=true | all-gather | bytes 655360 | tf_op jit(solution)/shard_map/all_gather | solution.py:148
  237.0 9.1 psum.163
  247.7 28.1 %reduce-scatter.22.cloned.1.call-done = f32[64,1,1024]{2,0,1:T(8,128)} async-done(((f32[256,1,1024]{2,0,1:T(8,128)}), f32[64,1,1024]{2,0,1:T(8,128)}) %reduce-scatter.22.cloned.1.call-update) | async-done | bytes 262160 | tf_op jit(solution)/shard_map/reduce_scatter | solution.py:172
  288.2 15.8 %all_gather.42 = bf16[256,1,1024]{2,0,1:T(8,128)(2,1)S(1)} all-gather(bf16[64,1,1024]{2,0,1:T(8,128)(2,1)S(1)} %multiply_convert_fusion.8), channel_id=1, replica_groups=mesh['section'=2,'dp'=4,'tensor'=4] {'tensor'}, dimensions={0}, use_global_device_ids=true | all-gather | bytes 655360 | tf_op jit(solution)/shard_map/all_gather | solution.py:148
  324.9 9.1 psum.164
  335.5 27.2 %reduce-scatter.24.cloned.1.call-done = f32[64,1,1024]{2,0,1:T(8,128)} async-done(((f32[256,1,1024]{2,0,1:T(8,128)}), f32[64,1,1024]{2,0,1:T(8,128)}) %reduce-scatter.24.cloned.1.call-update) | async-done | bytes 262160 | tf_op jit(solution)/shard_map/reduce_scatter | solution.py:172
  375.3 15.9 %all_gather.43 = bf16[256,1,1024]{2,0,1:T(8,128)(2,1)S(1)} all-gather(bf16[64,1,1024]{2,0,1:T(8,128)(2,1)S(1)} %multiply_convert_fusion.7), channel_id=1, replica_groups=mesh['section'=2,'dp'=4,'tensor'=4] {'tensor'}, dimensions={0}, use_global_device_ids=true | all-gather | bytes 655360 | tf_op jit(solution)/shard_map/all_gather | solution.py:148
  417.7 9.0 psum.165
  431.5 25.7 %reduce-scatter.26.cloned.1.call-done = f32[64,1,1024]{2,0,1:T(8,128)} async-done(((f32[256,1,1024]{2,0,1:T(8,128)}), f32[64,1,1024]{2,0,1:T(8,128)}) %reduce-scatter.26.cloned.1.call-update) | async-done | bytes 262160 | tf_op jit(solution)/shard_map/reduce_scatter | solution.py:172
  463.2 16.1 %all_gather.45 = bf16[256,1,1024]{2,0,1:T(8,128)(2,1)} all-gather(bf16[64,1,1024]{2,0,1:T(8,128)(2,1)} %bitcast_convert_fusion), channel_id=1, replica_groups=mesh['section'=2,'dp'=4,'tensor'=4] {'tensor'}, dimensions={0}, use_global_device_ids=true | all-gather | bytes 655360 | tf_op jit(solution)/shard_map/all_gather | solution.py:207
  483.1 15.1 %all_gather.44 = bf16[256,1,1024]{2,0,1:T(8,128)(2,1)S(1)} all-gather(bf16[64,1,1024]{2,0,1:T(8,128)(2,1)S(1)} %multiply_convert_fusion.6), channel_id=1, replica_groups=mesh['section'=2,'dp'=4,'tensor'=4] {'tensor'}, dimensions={0}, use_global_device_ids=true | all-gather | bytes 655360 | tf_op jit(solution)/shard_map/all_gather | solution.py:148
  531.5 10.8 psum.166
  546.7 9.7 psum.167
  614.9 28.0 %all-reduce.183 = bf16[256,1,256]{2,0,1:T(8,128)(2,1)} all-reduce(f32[256,1,256]{2,0,1:T(8,128)} %pad_add_fusion.29), channel_id=1, replica_groups=mesh['section'=2,'dp'=4,'tensor'=4] {'tensor'}, use_global_device_ids=true, to_apply=%region_48.50 | all-reduce | flops 65536 | bytes 393216 | tf_op jit(solution)/shard_map/psum | solution.py:229
  656.2 14.8 %all_gather.46 = bf16[256,1,1024]{2,0,1:T(8,128)(2,1)S(1)} all-gather(bf16[64,1,1024]{2,0,1:T(8,128)(2,1)S(1)} %fusion.612), channel_id=1, replica_groups=mesh['section'=2,'dp'=4,'tensor'=4] {'tensor'}, dimensions={0}, use_global_device_ids=true | all-gather | bytes 655360 | tf_op jit(solution)/shard_map/all_gather | solution.py:207
  674.8 11.5 psum.169
  696.7 5.4 fusion.180
  738.0 26.1 %all-reduce.184 = bf16[256,1,256]{2,0,1:T(8,128)(2,1)} all-reduce(f32[256,1,256]{2,0,1:T(8,128)} %pad_add_fusion.28), channel_id=1, replica_groups=mesh['section'=2,'dp'=4,'tensor'=4] {'tensor'}, use_global_device_ids=true, to_apply=%region_62.64 | all-reduce | flops 65536 | bytes 393216 | tf_op jit(solution)/shard_map/psum | solution.py:229
  770.8 5.5 collective-permute-done.6
  777.4 14.8 %all_gather.47 = bf16[256,1,1024]{2,0,1:T(8,128)(2,1)S(1)} all-gather(bf16[64,1,1024]{2,0,1:T(8,128)(2,1)S(1)} %fusion.613), channel_id=1, replica_groups=mesh['section'=2,'dp'=4,'tensor'=4] {'tensor'}, dimensions={0}, use_global_device_ids=true | all-gather | bytes 655360 | tf_op jit(solution)/shard_map/all_gather | solution.py:207
  794.9 11.8 psum.171
  817.0 5.4 fusion.182
  856.8 26.1 %all-reduce.185 = bf16[256,1,256]{2,0,1:T(8,128)(2,1)} all-reduce(f32[256,1,256]{2,0,1:T(8,128)} %pad_add_fusion.27), channel_id=1, replica_groups=mesh['section'=2,'dp'=4,'tensor'=4] {'tensor'}, use_global_device_ids=true, to_apply=%region_76.78 | all-reduce | flops 65536 | bytes 393216 | tf_op jit(solution)/shard_map/psum | solution.py:229
  889.0 6.1 collective-permute-done.7
  896.3 15.0 %all_gather.48 = bf16[256,1,1024]{2,0,1:T(8,128)(2,1)S(1)} all-gather(bf16[64,1,1024]{2,0,1:T(8,128)(2,1)S(1)} %fusion.614), channel_id=1, replica_groups=mesh['section'=2,'dp'=4,'tensor'=4] {'tensor'}, dimensions={0}, use_global_device_ids=true | all-gather | bytes 655360 | tf_op jit(solution)/shard_map/all_gather | solution.py:207
  913.9 11.3 psum.173
  935.5 5.4 fusion.184
  973.5 26.8 %all-reduce.186 = bf16[256,1,256]{2,0,1:T(8,128)(2,1)} all-reduce(f32[256,1,256]{2,0,1:T(8,128)} %pad_add_fusion.26), channel_id=1, replica_groups=mesh['section'=2,'dp'=4,'tensor'=4] {'tensor'}, use_global_device_ids=true, to_apply=%region_90.92 | all-reduce | flops 65536 | bytes 393216 | tf_op jit(solution)/shard_map/psum | solution.py:229
  1006.6 6.2 collective-permute-done.8
  1013.9 14.9 %all_gather.49 = bf16[256,1,1024]{2,0,1:T(8,128)(2,1)S(1)} all-gather(bf16[64,1,1024]{2,0,1:T(8,128)(2,1)S(1)} %fusion.615), channel_id=1, replica_groups=mesh['section'=2,'dp'=4,'tensor'=4] {'tensor'}, dimensions={0}, use_global_device_ids=true | all-gather | bytes 655360 | tf_op jit(solution)/shard_map/all_gather | solution.py:207
  1031.5 11.2 psum.175
  1107.5 25.9 %all-reduce.187 = bf16[256,1,256]{2,0,1:T(8,128)(2,1)} all-reduce(f32[256,1,256]{2,0,1:T(8,128)} %pad_add_fusion.25), channel_id=1, replica_groups=mesh['section'=2,'dp'=4,'tensor'=4] {'tensor'}, use_global_device_ids=true, to_apply=%region_104.106 | all-reduce | flops 65536 | bytes 393216 | tf_op jit(solution)/shard_map/psum | solution.py:229
  1139.6 6.1 collective-permute-done.9
  1145.7 14.8 %all_gather.50 = bf16[256,1,1024]{2,0,1:T(8,128)(2,1)S(1)} all-gather(bf16[64,1,1024]{2,0,1:T(8,128)(2,1)S(1)} %select_convert_fusion), channel_id=1, replica_groups=mesh['section'=2,'dp'=4,'tensor'=4] {'tensor'}, dimensions={0}, use_global_device_ids=true | all-gather | bytes 655360 | tf_op jit(solution)/shard_map/all_gather | solution.py:207
  1163.6 9.5 psum.177
  1222.2 24.9 %all-reduce.188 = bf16[256,1,256]{2,0,1:T(8,128)(2,1)S(1)} all-reduce(f32[256,1,256]{2,0,1:T(8,128)} %pad_add_fusion.20), channel_id=1, replica_groups=mesh['section'=2,'dp'=4,'tensor'=4] {'tensor'}, use_global_device_ids=true, to_apply=%region_118.120 | all-reduce | flops 65536 | bytes 393216 | tf_op jit(solution)/shard_map/psum | solution.py:229
  1264.2 12.2 slice_add_fusion
  1286.3 60.2 %all-reduce.176 = (f32[1,1024]{1,0:T(1,128)}, f32[5,2048]{1,0:T(8,128)S(1)}, f32[1,5,256]{2,0,1:T(1,128)}, f32[3,32]{1,0:T(4,128)S(1)}, f32[2048]{0:T(1024)S(1)}) all-reduce(f32[1,1024]{1,0:T(1,128)S(1)} %bitcast.2068, ...), channel_id=1, replica_groups=mesh['section'=2,'dp'=4,'tensor'=4] {'dp','tensor'}, use_global_device_ids=true, to_apply=%region_126.128 | all-reduce | flops 14688 | bytes 117504 | tf_op jit(solution)/shard_map/psum | solution.py:293
  1353.6 8.4 reduce-scatter.44.cloned.1.call-done
  1362.0 34.4 %reduce-scatter.42.cloned.1.call-done = f32[256,512]{1,0:T(8,128)} async-done(((f32[1024,512]{1,0:T(8,128)}), f32[256,512]{1,0:T(8,128)}) %reduce-scatter.42.cloned.1.call-update) | async-done | bytes 524304 | tf_op jit(solution)/shard_map/reduce_scatter | solution.py:276
  (1551 shorter events, 612.9 us)
Async XLA Ops:
  7.2 42.6 %all-gather.9.cloned.1.call-start = ((), (), s32[]{:S(2)}) async-start(), calls=%async_computation.29 | async-start | bytes 1310720 | tf_op jit(solution)/shard_map/all_gather | solution.py:115
  7.9 42.0 %all-gather.11.cloned.1.call-start = ((), (), s32[]{:S(2)}) async-start(), calls=%async_computation.30 | async-start | bytes 1310720 | tf_op jit(solution)/shard_map/all_gather | solution.py:116
  8.7 69.2 %all-gather.13.cloned.1.call-start = ((), (), s32[]{:S(2)}) async-start(), calls=%async_computation.31 | async-start | bytes 1310720 | tf_op jit(solution)/shard_map/all_gather | solution.py:119
  9.5 95.6 %reduce-scatter.18.cloned.1.call-start = ((), (), s32[]{:S(2)}) async-start(), calls=%async_computation.17 | async-start | bytes 1310720 | tf_op jit(solution)/shard_map/reduce_scatter | solution.py:172
  11.4 205.8 %copy-start.348 = (f32[8]{0:T(128)}, f32[8]{0:T(128)S(1)}, u32[]{:S(2)}) copy-start(f32[8]{0:T(128)S(1)} %get-tuple-element.421) | copy-start | bytes 100
  19.0 181.1 %copy-start.19 = (f32[1,5,64,1024]{3,2,1,0:T(8,128)}, f32[1,5,64,1024]{3,2,1,0:T(8,128)S(1)}, u32[]{:S(2)}) copy-start(f32[1,5,64,1024]{3,2,1,0:T(8,128)S(1)} %convert_element_type.124) | copy-start | bytes 3932164
  39.8 184.9 %copy-start.299 = (f32[1,1,256]{2,0,1:T(1,128)}, f32[1,1,256]{2,0,1:T(1,128)S(1)}, u32[]{:S(2)}) copy-start(f32[1,1,256]{2,0,1:T(1,128)S(1)} %get-tuple-element.409) | copy-start | bytes 3076
  39.8 274.3 %copy-start.260 = (f32[1,1,512]{2,0,1:T(1,128)}, f32[1,1,512]{2,0,1:T(1,128)S(1)}, u32[]{:S(2)}) copy-start(f32[1,1,512]{2,0,1:T(1,128)S(1)} %get-tuple-element.392) | copy-start | bytes 6148
  49.8 60.4 %copy-start.275 = (f32[256,8]{0,1:T(8,128)}, f32[256,8]{0,1:T(8,128)S(1)}, u32[]{:S(2)}) copy-start(f32[256,8]{0,1:T(8,128)S(1)} %get-tuple-element.407) | copy-start | bytes 24580
  80.6 108.6 %reduce-scatter.20.cloned.1.call-start = ((), (), s32[]{:S(2)}) async-start(), calls=%async_computation.18 | async-start | bytes 1310720 | tf_op jit(solution)/shard_map/reduce_scatter | solution.py:172
  81.4 59.2 %copy-start.272 = (f32[3,1,512]{2,0,1:T(4,128)}, f32[3,1,512]{2,0,1:T(4,128)S(1)}, u32[]{:S(2)}) copy-start(f32[3,1,512]{2,0,1:T(4,128)S(1)} %slice_select_fusion.6) | copy-start | bytes 18436
  106.1 8.8 collective-permute-start
  136.3 58.8 %copy-start.368 = (f32[8]{0:T(128)}, f32[8]{0:T(128)S(1)}, u32[]{:S(2)}) copy-start(f32[8]{0:T(128)S(1)} %slice_reduce_fusion.16) | copy-start | bytes 100
  137.2 57.9 %copy-start.277 = (f32[256,8]{0,1:T(8,128)}, f32[256,8]{0,1:T(8,128)S(1)}, u32[]{:S(2)}) copy-start(f32[256,8]{0,1:T(8,128)S(1)} %get-tuple-element.405) | copy-start | bytes 24580
  161.9 114.0 %reduce-scatter.22.cloned.1.call-start = ((), (), s32[]{:S(2)}) async-start(), calls=%async_computation.19 | async-start | bytes 1310720 | tf_op jit(solution)/shard_map/reduce_scatter | solution.py:172
  191.1 9.0 collective-permute-start.1
  223.0 87.0 %copy-start.292 = (f32[3,1,256]{2,0,1:T(4,128)}, f32[3,1,256]{2,0,1:T(4,128)S(1)}, u32[]{:S(2)}) copy-start(f32[3,1,256]{2,0,1:T(4,128)S(1)} %get-tuple-element.289) | copy-start | bytes 9220
  223.8 175.2 %copy-start.254 = (f32[3,1,512]{2,0,1:T(4,128)}, f32[3,1,512]{2,0,1:T(4,128)S(1)}, u32[]{:S(2)}) copy-start(f32[3,1,512]{2,0,1:T(4,128)S(1)} %get-tuple-element.293) | copy-start | bytes 18436
  224.7 56.3 %copy-start.279 = (f32[256,8]{0,1:T(8,128)}, f32[256,8]{0,1:T(8,128)S(1)}, u32[]{:S(2)}) copy-start(f32[256,8]{0,1:T(8,128)S(1)} %get-tuple-element.403) | copy-start | bytes 24580
  247.7 115.0 %reduce-scatter.24.cloned.1.call-start = ((), (), s32[]{:S(2)}) async-start(), calls=%async_computation.20 | async-start | bytes 1310720 | tf_op jit(solution)/shard_map/reduce_scatter | solution.py:172
  277.6 8.7 collective-permute-start.2
  287.4 75.2 %copy-start.46 = (f32[64,1,1024]{2,0,1:T(8,128)}, f32[64,1,1024]{2,0,1:T(8,128)S(1)}, u32[]{:S(2)}) copy-start(f32[64,1,1024]{2,0,1:T(8,128)S(1)} %get-tuple-element.296) | copy-start | bytes 786436
  310.0 58.5 %copy-start.283 = (f32[256,8]{0,1:T(8,128)}, f32[256,8]{0,1:T(8,128)S(1)}, u32[]{:S(2)}) copy-start(f32[256,8]{0,1:T(8,128)S(1)} %get-tuple-element.401) | copy-start | bytes 24580
  335.5 121.7 %reduce-scatter.26.cloned.1.call-start = ((), (), s32[]{:S(2)}) async-start(), calls=%async_computation.21 | async-start | bytes 1310720 | tf_op jit(solution)/shard_map/reduce_scatter | solution.py:172
  364.5 9.0 collective-permute-start.3
  400.6 78.7 %copy-start.382 = (f32[8]{0:T(128)}, f32[8]{0:T(128)S(1)}, u32[]{:S(2)}) copy-start(f32[8]{0:T(128)S(1)} %slice_reduce_fusion.13) | copy-start | bytes 100
  429.9 213.0 %reduce-scatter.30.cloned.1.call-start = ((), (), s32[]{:S(2)}) async-start(), calls=%async_computation.23 | async-start | bytes 1310720 | tf_op jit(solution)/shard_map/reduce_scatter | solution.py:248
  459.2 23.0 %collective-permute-start.4 = (f32[64,1,1024]{2,0,1:T(8,128)}, f32[64,1,1024]{2,0,1:T(8,128)}, u32[]{:S(2)}, u32[]{:S(2)}) collective-permute-start(f32[64,1,1024]{2,0,1:T(8,128)} %get-tuple-element.270), channel_id=1, source_target_pairs={{0,16},{1,17},{2,18},{3,19},{4,20},{5,21},{6,22},{7,23},{8,24},{9,... | collective-permute-start | bytes 786440 | tf_op jit(solution)/shard_map/ppermute | solution.py:21
  607.0 157.1 %reduce-scatter.32.cloned.1.call-start = ((), (), s32[]{:S(2)}) async-start(), calls=%async_computation.24 | async-start | bytes 1310720 | tf_op jit(solution)/shard_map/reduce_scatter | solution.py:248
  646.6 8.6 collective-permute-start.5
  730.0 153.0 %reduce-scatter.34.cloned.1.call-start = ((), (), s32[]{:S(2)}) async-start(), calls=%async_computation.25 | async-start | bytes 1310720 | tf_op jit(solution)/shard_map/reduce_scatter | solution.py:248
  767.8 8.5 collective-permute-start.6
  849.9 150.5 %reduce-scatter.36.cloned.1.call-start = ((), (), s32[]{:S(2)}) async-start(), calls=%async_computation.26 | async-start | bytes 1310720 | tf_op jit(solution)/shard_map/reduce_scatter | solution.py:248
  886.7 8.5 collective-permute-start.7
  967.8 165.5 %reduce-scatter.38.cloned.1.call-start = ((), (), s32[]{:S(2)}) async-start(), calls=%async_computation.27 | async-start | bytes 1310720 | tf_op jit(solution)/shard_map/reduce_scatter | solution.py:248
  970.6 106.6 %copy-start.318 = (f32[3,1,256]{2,0,1:T(4,128)}, f32[3,1,256]{2,0,1:T(4,128)S(1)}, u32[]{:S(2)}) copy-start(f32[3,1,256]{2,0,1:T(4,128)S(1)} %add_select_fusion.6) | copy-start | bytes 9220
  1004.2 8.6 collective-permute-start.8
  1085.0 192.5 %reduce-scatter.28.cloned.1.call-start = ((), (), s32[]{:S(2)}) async-start(), calls=%async_computation.22 | async-start | bytes 1310720 | tf_op jit(solution)/shard_map/reduce_scatter | solution.py:172
  1095.7 189.1 %reduce-scatter.40.cloned.1.call-start = ((), (), s32[]{:S(2)}) async-start(), calls=%async_computation.28 | async-start | bytes 1310720 | tf_op jit(solution)/shard_map/reduce_scatter | solution.py:248
  1137.1 8.6 collective-permute-start.9
  1207.5 146.1 %reduce-scatter.48.cloned.1.call-start = ((), (), s32[]{:S(2)}) async-start(), calls=%async_computation.35 | async-start | bytes 40960 | tf_op jit(solution)/shard_map/reduce_scatter | solution.py:281
  1247.2 106.4 %reduce-scatter.46.cloned.1.call-start = ((), (), s32[]{:S(2)}) async-start(), calls=%async_computation.34 | async-start | bytes 1310720 | tf_op jit(solution)/shard_map/reduce_scatter | solution.py:280
  1255.6 98.0 %reduce-scatter.50.cloned.1.call-start = ((), (), s32[]{:S(2)}) async-start(), calls=%async_computation.36 | async-start | bytes 2621440 | tf_op jit(solution)/shard_map/reduce_scatter | solution.py:282
  1264.1 97.9 %reduce-scatter.44.cloned.1.call-start = ((), (), s32[]{:S(2)}) async-start(), calls=%async_computation.33 | async-start | bytes 2621440 | tf_op jit(solution)/shard_map/reduce_scatter | solution.py:277
  1276.7 119.7 %reduce-scatter.42.cloned.1.call-start = ((), (), s32[]{:S(2)}) async-start(), calls=%async_computation.32 | async-start | bytes 2621440 | tf_op jit(solution)/shard_map/reduce_scatter | solution.py:276
  1277.3 71.0 %copy-start.225 = (f32[64,1,1024]{2,0,1:T(8,128)S(1)}, f32[64,1,1024]{2,0,1:T(8,128)}, u32[]{:S(2)}) copy-start(f32[64,1,1024]{2,0,1:T(8,128)} %copy-done.224) | copy-start | bytes 786436
  1279.5 68.8 %copy-start.462 = (f32[64]{0:T(128)S(1)}, f32[64]{0:T(128)}, u32[]{:S(2)}) copy-start(f32[64]{0:T(128)} %copy-done.461) | copy-start | bytes 772
  1279.7 68.6 %copy-start.478 = (f32[64]{0:T(128)S(1)}, f32[64]{0:T(128)}, u32[]{:S(2)}) copy-start(f32[64]{0:T(128)} %get-tuple-element.423) | copy-start | bytes 772
  (483 other events, 3572.0 us)
Sparse Core Ops, SparseCore 0:
  9.6 19.4 all-gather.8
  30.6 19.2 all-gather.10
  52.1 16.3 all-gather.12
  80.7 24.3 reduce-scatter.17
  162.0 27.1 reduce-scatter.19
  247.8 28.0 reduce-scatter.21
  335.6 27.0 reduce-scatter.23
  430.0 27.1 reduce-scatter.25
  607.2 30.9 reduce-scatter.29
  730.1 29.3 reduce-scatter.31
  850.0 28.4 reduce-scatter.33
  967.9 27.6 reduce-scatter.35
  1085.1 26.7 reduce-scatter.37
  1114.0 29.7 reduce-scatter.27
  1207.6 29.3 reduce-scatter.39
  1247.3 17.0 reduce-scatter.47
  1267.5 24.8 reduce-scatter.45
  1295.4 31.8 reduce-scatter.49
  1330.6 31.3 reduce-scatter.43
  1364.9 31.3 reduce-scatter.41
where the time goes:
time: 1420 us; the launch traced here: 1400 us
  blocking collectives  544 us (38%)
  matrix products  254 us (18%)
  other arithmetic  243 us (17%)
  waiting for transfers between devices  216 us (15%)
  local copies, waits for them, and re-layouts  101 us (7%)
  starting transfers between devices  26.3 us (2%)
  between operations  19.8 us (1%)
    psum x6, blocking collectives, per_device(): state_total = lax.psum(grad_proj[..., 2 * width_loc:], 'tensor')  158 us
    reduce_scatter x6, waiting for transfers between devices, per_device(): lax.psum_scatter(jnp.einsum('tbc,cd->tbd', normed_gate, out_weights, pref...  132 us
    psum x12, blocking collectives, head_total(): return lax.psum(values, 'tensor')  124 us
    all_gather x6, blocking collectives, per_device(): normed_full = lax.all_gather(normed, 'tensor', axis=0, tiled=True)  95.6 us
    all_gather x6, blocking collectives, per_device(): grad_full = lax.all_gather(grad_low, 'tensor', axis=0, tiled=True)  90.4 us
    dot_general x18, matrix products, ssd_block(): jnp.einsum('bhts,sbhp->tbhp', mixing, x_heads, precision=FULL_PRECISION)  79.1 us
    psum x1, blocking collectives, per_device(): lax.psum((gain_in_acc, place_local(taps_inner_acc, INNER), taps_state_acc...  60.2 us
    ppermute x10, waiting for transfers between devices, shifted(): return lax.ppermute(block, axis, route)  38.7 us
  transfers between devices with their start and end apart: 30, of which 17 were waited for; matrix products, arithmetic and copies ran while one was open for 13% of the time, Pallas kernels for 0%

commit v1 on v0

v1 whole, which is shorter than its diff:
```python
import jax
import jax.numpy as jnp
from jax import lax
from jax.sharding import PartitionSpec as P

D = 1024
HEADS = 32
HEADDIM = 64
STATE = 128
CONV = 4
INNER = 2048
CHUNK = 128
SIDE = 128

EPSILON = 1e-05
EXACT = lax.Precision.HIGHEST
FULL_PRECISION = lax.Precision.HIGH
LINK = jnp.float32


def shifted(block, distance):
    route = [(0, 1)] if distance == 1 else [(1, 0)]
    return lax.ppermute(block, "section", route)


def causal_conv(padded, tap_rows):
    rows = padded.shape[1] - CONV + 1
    summed = tap_rows[CONV]
    for offset in range(CONV):
        summed = summed + tap_rows[offset] * padded[:, offset : offset + rows]
    return summed


def with_history(values, tail, first_section, overlap):
    history = jnp.pad(tail, ((0, 0), (overlap - CONV + 1, 0), (0, 0)))
    top = jnp.where(first_section, values[:, :overlap], history)
    return jnp.concatenate([jnp.zeros_like(tail), top, values[:, overlap:]], 1)


def ssd(x_act, b_in, c_out, step, rate, skip):
    seqs, rows, heads = step.shape
    chunks = rows // CHUNK
    x_heads = x_act.reshape(seqs, chunks, CHUNK, heads, HEADDIM)
    b_c = b_in.reshape(seqs, chunks, CHUNK, STATE)
    c_c = c_out.reshape(seqs, chunks, CHUNK, STATE)
    step_c = jnp.transpose(step.reshape(seqs, chunks, CHUNK, heads), (0, 1, 3, 2))
    log_decay = step_c * rate[:, None]
    mask = lax.broadcasted_iota(jnp.int32, (CHUNK, CHUNK), 0) >= lax.broadcasted_iota(
        jnp.int32, (CHUNK, CHUNK), 1
    )
    running = jnp.einsum("bchs,ts->bcht", log_decay, mask.astype(jnp.float32), precision=EXACT)
    total = running[..., -1]
    spread = running[..., :, None] - running[..., None, :]
    kernel = jnp.where(mask, jnp.exp(jnp.where(mask, spread, 0.0)), 0.0)
    weighting = jnp.exp(total[..., None] - running) * step_c
    added = jnp.einsum(
        "bcshp,bcsn->bchpn",
        x_heads * jnp.transpose(weighting, (0, 1, 3, 2))[..., None],
        b_c,
        precision=FULL_PRECISION,
    )
    fade = jnp.exp(total)[..., None, None]
    held = jnp.zeros_like(added[:, 0])
    before = []
    for chunk in range(chunks):
        before.append(held)
        held = fade[:, chunk] * held + added[:, chunk]
    arrived = shifted(held, 1)
    scores = jnp.einsum("bctn,bcsn->bcts", c_c, b_c, precision=FULL_PRECISION)
    mixing = scores[:, :, None] * kernel * step_c[..., None, :]
    inside = jnp.einsum("bchts,bcshp->bcthp", mixing, x_heads, precision=FULL_PRECISION)
    entering = []
    for chunk in range(chunks):
        entering.append(before[chunk] + arrived)
        arrived = fade[:, chunk] * arrived
    carried_out = jnp.einsum(
        "bctn,bchpn->bcthp", c_c, jnp.stack(entering, 1), precision=FULL_PRECISION
    )
    outputs = (
        inside
        + carried_out * jnp.transpose(jnp.exp(running), (0, 1, 3, 2))[..., None]
        + skip[:, None] * x_heads
    )
    return outputs.reshape(x_act.shape)


def mixer(
    gate_part, inner_part, state_part, step_raw, taps_inner, taps_state, head_rows,
    first_section, row_valid, overlap,
):
    tails = shifted(
        jnp.concatenate([inner_part[:, 1 - CONV :], state_part[:, 1 - CONV :]], 2), 1
    )
    width = inner_part.shape[2]
    inner_rows = with_history(inner_part, tails[..., :width], first_section, overlap)
    state_rows = with_history(state_part, tails[..., width:], first_section, overlap)
    x_act = jax.nn.silu(causal_conv(inner_rows, taps_inner))
    state_act = jax.nn.silu(causal_conv(state_rows, taps_state))
    step = jnp.where(row_valid, jax.nn.softplus(step_raw + head_rows[0]), 0.0)
    head_out = ssd(
        x_act,
        state_act[..., :STATE],
        state_act[..., STATE:],
        step,
        -jnp.exp(head_rows[1]),
        head_rows[2],
    )
    return jnp.where(row_valid, head_out * jax.nn.silu(gate_part), 0.0)


def per_device(
    tokens,
    cotangent,
    norm_gain,
    gate_weight,
    inner_weight,
    state_weight,
    step_weight,
    conv_inner,
    conv_state,
    head_params,
    gate_gain,
    out_weight,
):
    tensor_rank = lax.axis_index("tensor")
    section_rank = lax.axis_index("section")
    ranks = lax.axis_size("tensor")
    first_section = section_rank == 0
    seqs, block_count, part_rows, _ = tokens.shape
    held_blocks = (block_count + 1) // 2
    group = part_rows * ranks
    rows = held_blocks * group
    overlap = (2 * held_blocks - block_count) * group
    width = gate_weight.shape[2]
    heads_loc = step_weight.shape[2]
    row_valid = first_section | (
        lax.broadcasted_iota(jnp.int32, (1, rows, 1), 1) >= overlap
    )
    block_valid = first_section | (
        lax.broadcasted_iota(jnp.int32, (1, held_blocks, 1, 1), 1) >= 2 * held_blocks - block_count
    )

    def both_layers(values):
        gathered = lax.all_gather(values, ("section", "dp"), axis=0, tiled=False)
        return gathered.reshape(2, -1, values.shape[-1])

    in_weights = both_layers(
        jnp.concatenate([gate_weight[0], inner_weight[0], state_weight[0], step_weight[0]], 1)
    )
    out_local = lax.dynamic_slice_in_dim(out_weight[0], tensor_rank * width, width, 0)
    out_weights_t = both_layers(out_local.T)
    small_in = lax.all_gather(
        jnp.concatenate(
            [
                norm_gain[0],
                lax.dynamic_slice_in_dim(gate_gain[0], tensor_rank * width, width, 0),
                conv_inner[0].reshape(-1),
                conv_state[0].reshape(-1),
                head_params[0].reshape(-1),
            ]
        ),
        "section",
        axis=0,
        tiled=False,
    )

    def split_small(vector):
        sizes = (
            (D,),
            (width,),
            (CONV + 1, width),
            (CONV + 1, 2 * STATE),
            (3, heads_loc),
        )
        parts, at = [], 0
        for size in sizes:
            count = size[0] * (size[1] if len(size) > 1 else 1)
            parts.append(vector[at : at + count].reshape(size))
            at += count
        return parts

    def spread_rows(values):
        gathered = lax.all_gather(values, "tensor", axis=0, tiled=False)
        return jnp.transpose(gathered, (1, 2, 0, 3, 4)).reshape(seqs, rows, values.shape[-1])

    def by_rank(values):
        split = values.reshape(seqs, held_blocks, ranks, part_rows, values.shape[-1])
        return jnp.transpose(split, (2, 0, 1, 3, 4))

    def row_sums(partial):
        return lax.psum_scatter(
            partial.astype(LINK), "tensor", scatter_dimension=0, tiled=False
        ).astype(jnp.float32)

    def forward(hidden, layer):
        gain_rows, gate_scale, taps_inner, taps_state, head_rows = split_small(small_in[layer])
        proj, out_t = in_weights[layer], out_weights_t[layer]
        inv_rms = lax.rsqrt(jnp.mean(hidden * hidden, axis=3, keepdims=True) + EPSILON)
        normed = spread_rows((hidden * inv_rms * gain_rows).astype(jnp.bfloat16))
        raw = jnp.einsum("btd,dc->btc", normed, proj, preferred_element_type=jnp.float32)
        gate_out, pullback = jax.vjp(
            lambda *parts: mixer(*parts, first_section, row_valid, overlap),
            raw[..., :width],
            raw[..., width : 2 * width],
            raw[..., 2 * width : 2 * width + 2 * STATE],
            raw[..., 2 * width + 2 * STATE :],
            taps_inner,
            taps_state,
            head_rows,
        )
        scaled = (gate_out * gate_scale).astype(jnp.bfloat16)
        partial = jnp.einsum(
            "kbgqc,dc->kbgqd", by_rank(scaled), out_t, preferred_element_type=jnp.float32
        )
        squares = by_rank(jnp.sum(gate_out * gate_out, axis=2, keepdims=True))
        squares = jnp.pad(squares, ((0, 0),) * 4 + ((0, SIDE - 1),))
        summed = row_sums(jnp.concatenate([partial, squares], 4))
        inv_gate = lax.rsqrt(summed[..., D : D + 1] / INNER + EPSILON)
        branch = inv_gate * summed[..., :D]
        kept = (hidden, inv_rms, normed, pullback, gate_out, scaled, inv_gate, branch)
        return hidden + branch, kept

    def backward(grad_out, layer, kept):
        hidden, inv_rms, normed, pullback, gate_out, scaled, inv_gate, branch = kept
        gain_rows, gate_scale = split_small(small_in[layer])[:2]
        proj, out_t = in_weights[layer], out_weights_t[layer]
        pull = inv_gate * inv_gate * jnp.sum(grad_out * branch, axis=3, keepdims=True) / INNER
        pull_high = pull.astype(jnp.bfloat16)
        pull_low = (pull - pull_high.astype(jnp.float32)).astype(jnp.bfloat16)
        side = jnp.pad(
            jnp.concatenate([pull_high, pull_low], 3), ((0, 0),) * 3 + ((0, SIDE - 2),)
        )
        full = spread_rows(
            jnp.concatenate([(inv_gate * grad_out).astype(jnp.bfloat16), side], 3)
        )
        upper = full[..., :D]
        pull_full = full[..., D : D + 1].astype(jnp.float32) + full[..., D + 1 : D + 2].astype(
            jnp.float32
        )
        through = jnp.einsum("btd,dc->btc", upper, out_t, preferred_element_type=jnp.float32)
        out_grad = jnp.einsum("btd,btc->dc", upper, scaled, preferred_element_type=jnp.float32)
        out_grad = lax.psum_scatter(out_grad, "dp", scatter_dimension=0, tiled=True)
        gate_gain_grad = jnp.sum(through * gate_out, axis=(0, 1))
        parts = pullback(gate_scale * through - gate_out * pull_full)
        low = jnp.concatenate([part.astype(jnp.bfloat16) for part in parts[:4]], 2)
        grad_normed = row_sums(
            jnp.einsum("kbgqc,dc->kbgqd", by_rank(low), proj, preferred_element_type=jnp.float32)
        )
        proj_grad = jnp.einsum("btd,btc->dc", normed, low, preferred_element_type=jnp.float32)
        proj_grad = lax.psum_scatter(proj_grad, "dp", scatter_dimension=0, tiled=True)
        norm_gain_grad = jnp.sum(grad_normed * hidden * inv_rms, axis=(0, 1, 2))
        inner_in = jnp.sum(grad_normed * gain_rows * hidden, axis=3, keepdims=True)
        grad_in = grad_out + inv_rms * gain_rows * grad_normed - hidden * inv_rms**3 * inner_in / D
        weight_grads = jnp.concatenate([proj_grad, out_grad], 1)
        shared = jnp.concatenate([norm_gain_grad, parts[5].reshape(-1)])
        own = jnp.concatenate([gate_gain_grad, parts[4].reshape(-1), parts[6].reshape(-1)])
        return grad_in, weight_grads, shared, own

    first_block = jnp.where(first_section, 0, block_count - held_blocks)

    def held(values):
        return lax.dynamic_slice_in_dim(values, first_block, held_blocks, 1)

    extra = 2 * held_blocks - block_count

    def joined(in_first, in_second, to_first, to_second):
        return jnp.where(
            first_section,
            jnp.concatenate([in_first, to_first], 1),
            jnp.concatenate([to_second, in_second[:, extra:]], 1),
        )

    middle, kept_first = forward(held(tokens).astype(jnp.float32), 0)
    final, kept_second = forward(middle, 1)
    output = joined(middle, final, shifted(middle[:, extra:], -1), shifted(final, 1))

    top_grad = jnp.where(block_valid, held(cotangent), 0.0)
    grad_second, weights_second, shared_second, own_second = backward(top_grad, 1, kept_second)
    weights_to_second = shifted(weights_second, 1)
    grad_to_second = shifted(grad_second, 1)
    grad_first, weights_first, shared_first, own_first = backward(grad_second, 0, kept_first)
    weights_to_first = shifted(weights_first, -1)
    input_grad = joined(
        grad_first, grad_second, shifted(grad_first[:, extra:], -1), grad_to_second
    )
    weights = jnp.where(
        first_section, weights_first + weights_to_first, weights_second + weights_to_second
    )
    state_at = 2 * width
    step_at = state_at + 2 * STATE
    out_at = step_at + heads_loc
    state_grad = lax.psum(weights[:, state_at:step_at], "tensor")
    shared = lax.psum(jnp.stack([shared_first, shared_second]), ("section", "dp", "tensor"))
    own = lax.psum(jnp.stack([own_first, own_second]), ("section", "dp"))
    shared = jnp.where(first_section, shared[0], shared[1])
    own = jnp.where(first_section, own[0], own[1])
    taps_end = width * (CONV + 2)
    return (
        output[None],
        input_grad[None],
        shared[:D][None],
        weights[:, :width][None],
        weights[:, width:state_at][None],
        state_grad[None],
        weights[:, step_at:out_at][None],
        own[width:taps_end].reshape(1, CONV + 1, width),
        shared[D:].reshape(1, CONV + 1, 2 * STATE),
        own[taps_end:].reshape(1, 3, heads_loc),
        own[:width][None],
        weights[:, out_at:].T[None],
    )


def solution(mesh):
    return jax.shard_map(
        per_device,
        mesh=mesh,
        in_specs=(
            P("dp", None, "tensor", None),
            P("dp", None, "tensor", None),
            P("section", None),
            P("section", "dp", "tensor"),
            P("section", "dp", "tensor"),
            P("section", "dp", None),
            P("section", "dp", "tensor"),
            P("section", None, "tensor"),
            P("section", None, None),
            P("section", None, "tensor"),
            P("section", None),
            P("section", None, "dp"),
        ),
        out_specs=(
            P("section", "dp", None, "tensor", None),
            P("section", "dp", None, "tensor", None),
            P("section", None),
            P("section", "dp", "tensor"),
            P("section", "dp", "tensor"),
            P("section", "dp", None),
            P("section", "dp", "tensor"),
            P("section", None, "tensor"),
            P("section", None, None),
            P("section", None, "tensor"),
            P("section", "tensor"),
            P("section", "tensor", "dp"),
        ),
        check_vma=False,
    )
```

time: 1420 us -> 1270 us (0.89)
  waiting for transfers between devices: 216 us -> 690 us
  blocking collectives: 544 us -> 81.3 us
  matrix products: 254 us -> 129 us
  other arithmetic: 243 us -> 126 us
  local copies, waits for them, and re-layouts: 101 us -> 171 us
  starting transfers between devices: 26.3 us -> 43.2 us
    psum x19 -> x2, blocking collectives: 342 us -> 71.2 us  [the longest x1 48.2 us: per_device(): lax.psum(jnp.stack([shared_first, shared_second]), ('section', 'dp', 'ten...]
    reduce_scatter x17 -> x8, waiting for transfers between devices: 175 us -> 435 us  [the longest x4 435 us: row_sums(): lax.psum_scatter(partial.astype(LINK), 'tensor', scatter_dimension=0, til...]
    all_gather x14 -> x0, blocking collectives: 202 us -> none  [the longest x6 95.6 us: per_device(): normed_full = lax.all_gather(normed, 'tensor', axis=0, tiled=True)]
    all_gather x3 -> x6, waiting for transfers between devices: 0.11 us -> 180 us  [the longest x4 138 us: spread_rows(): gathered = lax.all_gather(values, 'tensor', axis=0, tiled=False)]
    dot_general x130 -> x40, matrix products: 254 us -> 129 us  [the longest x6 24.2 us: ssd(): jnp.einsum('bchts,bcshp->bcthp', mixing, x_heads, precision=FULL_PRECISION)]
    reduce_sum x54 -> x27, other arithmetic: 90 us -> 43.5 us  [the longest x4 12.7 us: causal_conv(): summed = summed + tap_rows[offset] * padded[:, offset:offset + rows]]
    another operation x48 -> x4, other arithmetic: 38.4 us -> 0.31 us  [the longest x2 0.26 us: ssd(): jnp.stack(entering, 1)]
    psum x0 -> x1, waiting for transfers between devices: none -> 28.8 us  [per_device(): state_grad = lax.psum(weights[:, state_at:step_at], 'tensor')]
  transfers between devices with their start and end apart: 30 -> 29, of which waited for: 17 -> 18; matrix products, arithmetic and copies ran while one was open for 13% -> 19% of each run, Pallas kernels for 0% -> 0%
where the time goes in v1:
time: 1270 us; the launch traced here: 1260 us
  waiting for transfers between devices  690 us (54%)
  local copies, waits for them, and re-layouts  171 us (13%)
  matrix products  129 us (10%)
  other arithmetic  126 us (10%)
  blocking collectives  81.3 us (6%)
  starting transfers between devices  43.2 us (3%)
  between operations  19.1 us (2%)
    reduce_scatter x4, waiting for transfers between devices, row_sums(): lax.psum_scatter(partial.astype(LINK), 'tensor', scatter_dimension=0, til...  435 us
    all_gather x4, waiting for transfers between devices, spread_rows(): gathered = lax.all_gather(values, 'tensor', axis=0, tiled=False)  138 us
    psum x1, blocking collectives, per_device(): lax.psum(jnp.stack([shared_first, shared_second]), ('section', 'dp', 'ten...  48.2 us
    ppermute x14, waiting for transfers between devices, shifted(): return lax.ppermute(block, 'section', route)  45.4 us
    unnamed x645, local copies, waits for them, and re-layouts  42.8 us
    all_gather x2, waiting for transfers between devices, both_layers(): gathered = lax.all_gather(values, ('section', 'dp'), axis=0, tiled=False)  41.9 us
    ppermute x14, starting transfers between devices, shifted(): return lax.ppermute(block, 'section', route)  41.6 us
    psum x1, waiting for transfers between devices, per_device(): state_grad = lax.psum(weights[:, state_at:step_at], 'tensor')  28.8 us
  transfers between devices with their start and end apart: 29, of which 18 were waited for; matrix products, arithmetic and copies ran while one was open for 19% of the time, Pallas kernels for 0%

profile of v1, /device:TPU:0, one launch (start us, length us, event | category | flops | bytes accessed | tf_op | source)
XLA Modules:
  0.0 1258.5 jit_solution(624424928588469256)
XLA Ops:
  12.4 10.1 all-reduce.106
  31.3 30.6 %all-gather.14.cloned.1.call-done = bf16[4,3,64,1024]{3,2,1,0:T(8,128)(2,1)} async-done(((bf16[1,3,64,1024]{3,2,1,0:T(8,128)(2,1)}), bf16[4,3,64,1024]{3,2,1,0:T(8,128)(2,1)}) %all-gather.14.cloned.1.call-update) | async-done | bytes 1572880 | tf_op jit(solution)/shard_map/all_gather | solution.py:183
  63.6 41.9 %all-gather.16.cloned.1.call-done = bf16[2048,1288]{0,1:T(8,128)(2,1)} async-done(((bf16[256,1288]{0,1:T(8,128)(2,1)}), bf16[2048,1288]{0,1:T(8,128)(2,1)}) %all-gather.16.cloned.1.call-update) | async-done | bytes 5275664 | tf_op jit(solution)/shard_map/all_gather | solution.py:144
  105.5 4.0 convolution_bitcast_fusion.1
  114.9 8.9 collective-permute-done
  140.5 4.6 collective-permute-start.1
  162.8 4.0 multiply_convert_fusion.4
  172.7 3.5 select_maximum_fusion.1
  176.3 125.4 %reduce-scatter.9.cloned.1.call-done = f32[1,1,3,64,1152]{3,4,2,1,0:T(8,128)} async-done(((f32[4,1,3,64,1152]{3,4,2,1,0:T(8,128)}), f32[1,1,3,64,1152]{3,4,2,1,0:T(8,128)}) %reduce-scatter.9.cloned.1.call-update) | async-done | bytes 884752 | tf_op jit(solution)/shard_map/reduce_scatter | solution.py:191
  308.7 37.3 %all-gather.20.cloned.1.call-done = bf16[4,3,64,1024]{3,2,1,0:T(8,128)(2,1)} async-done(((bf16[1,3,64,1024]{3,2,1,0:T(8,128)(2,1)}), bf16[4,3,64,1024]{3,2,1,0:T(8,128)(2,1)}) %all-gather.20.cloned.1.call-update) | async-done | bytes 1572880 | tf_op jit(solution)/shard_map/all_gather | solution.py:183
  347.6 4.6 convolution_bitcast_fusion
  360.2 3.9 collective-permute-done.3
  381.6 4.6 collective-permute-start.4
  406.7 3.8 multiply_convert_fusion.2
  420.3 3.5 select_maximum_fusion
  427.6 118.1 %reduce-scatter.11.cloned.1.call-done = f32[1,1,3,64,1152]{3,4,2,1,0:T(8,128)} async-done(((f32[4,1,3,64,1152]{3,4,2,1,0:T(8,128)}), f32[1,1,3,64,1152]{3,4,2,1,0:T(8,128)}) %reduce-scatter.11.cloned.1.call-update) | async-done | bytes 884752 | tf_op jit(solution)/shard_map/reduce_scatter | solution.py:191
  552.4 40.5 %all-gather.22.cloned.1.call-done = bf16[4,3,64,1152]{3,2,1,0:T(8,128)(2,1)} async-done(((bf16[1,3,64,1152]{3,2,1,0:T(8,128)(2,1)}), bf16[4,3,64,1152]{3,2,1,0:T(8,128)(2,1)}) %all-gather.22.cloned.1.call-update) | async-done | bytes 1769488 | tf_op jit(solution)/shard_map/all_gather | solution.py:183
  595.3 6.1 multiply_reduce_fusion.4
  615.4 6.2 fusion.29
  645.6 6.0 multiply_reduce_fusion.8
  676.3 5.6 collective-permute-done.7
  686.0 4.1 copy.439
  690.1 9.0 convolution_bitcast_fusion.3
  699.4 108.7 %reduce-scatter.13.cloned.1.call-done = f32[1,1,3,64,1024]{3,4,2,1,0:T(8,128)} async-done(((f32[4,1,3,64,1024]{3,4,2,1,0:T(8,128)}), f32[1,1,3,64,1024]{3,4,2,1,0:T(8,128)}) %reduce-scatter.13.cloned.1.call-update) | async-done | bytes 786448 | tf_op jit(solution)/shard_map/reduce_scatter | solution.py:191
  815.4 6.4 fusion.24
  822.9 3.7 fusion.117
  826.7 29.6 %all-gather.24.cloned.1.call-done = bf16[4,3,64,1152]{3,2,1,0:T(8,128)(2,1)} async-done(((bf16[1,3,64,1152]{3,2,1,0:T(8,128)(2,1)}), bf16[4,3,64,1152]{3,2,1,0:T(8,128)(2,1)}) %all-gather.24.cloned.1.call-update) | async-done | bytes 1769488 | tf_op jit(solution)/shard_map/all_gather | solution.py:183
  858.4 6.1 multiply_reduce_fusion.9
  879.2 6.2 fusion.31
  907.1 4.5 fusion.163
  927.1 8.5 collective-permute-done.9
  937.7 4.5 fusion.26
  943.3 3.7 fusion.119
  950.7 4.5 copy.459
  955.2 9.4 convolution_bitcast_fusion.2
  969.1 6.2 collective-permute-start.5
  975.3 5.0 collective-permute-done.2
  983.9 6.9 collective-permute-done.5
  996.3 5.3 collective-permute-start.11
  1001.6 3.6 maximum_select_fusion
  1009.8 6.4 collective-permute-done.11
  1021.4 22.9 %psum.23 = f32[2,3096]{1,0:T(2,128)S(1)} all-reduce(f32[2,3096]{1,0:T(2,128)S(1)} %pad_maximum_fusion.13), channel_id=1, replica_groups=mesh['section'=2,'dp'=4,'tensor'=4] {'section','dp'}, use_global_device_ids=true, to_apply=%region_86.88 | all-reduce | flops 6192 | bytes 49536 | tf_op jit(solution)/shard_map/psum | solution.py:294
  1050.7 5.4 collective-permute-start.13
  1061.8 83.0 %reduce-scatter.15.cloned.1.call-done = f32[1,1,3,64,1024]{3,4,2,1,0:T(8,128)} async-done(((f32[4,1,3,64,1024]{3,4,2,1,0:T(8,128)}), f32[1,1,3,64,1024]{3,4,2,1,0:T(8,128)}) %reduce-scatter.15.cloned.1.call-update) | async-done | bytes 786448 | tf_op jit(solution)/shard_map/reduce_scatter | solution.py:191
  1152.7 48.2 %psum.21 = f32[2,2304]{1,0:T(2,128)S(1)} all-reduce(f32[2,2304]{1,0:T(2,128)S(1)} %pad_maximum_fusion.14), channel_id=1, replica_groups=mesh['section'=2,'dp'=4,'tensor'=4] {'section','dp','tensor'}, use_global_device_ids=true, to_apply=%region_60.62 | all-reduce | flops 4608 | bytes 36864 | tf_op jit(solution)/shard_map/psum | solution.py:293
  1204.5 3.5 maximum_select_fusion.1
  1211.0 3.6 add_select_fusion
  1221.2 28.8 %all-reduce.109.cloned.1.call-done = f32[1,256,256]{1,2,0:T(8,128)} async-done(((f32[1,256,256]{1,2,0:T(8,128)}), f32[1,256,256]{1,2,0:T(8,128)}) %all-reduce.109.cloned.1.call-update) | async-done | bytes 262160 | tf_op jit(solution)/shard_map/psum | solution.py:292
  (974 shorter events, 328.6 us)
Async XLA Ops:
  7.2 416.7 %copy-start = (f32[1,5,64,1024]{3,2,1,0:T(8,128)S(1)}, f32[1,5,64,1024]{3,2,1,0:T(8,128)}, u32[]{:S(2)}) copy-start(f32[1,5,64,1024]{3,2,1,0:T(8,128)} %param.14) | copy-start | bytes 3932164
  7.2 54.7 %all-gather.14.cloned.1.call-start = ((), (), s32[]{:S(2)}) async-start(), calls=%async_computation.17 | async-start | bytes 1966080 | tf_op jit(solution)/shard_map/all_gather | solution.py:183
  24.5 81.0 %all-gather.16.cloned.1.call-start = ((), (), s32[]{:S(2)}) async-start(), calls=%async_computation.18 | async-start | bytes 5935104 | tf_op jit(solution)/shard_map/all_gather | solution.py:144
  26.8 142.7 %all-gather.18.cloned.1.call-start = ((), (), s32[]{:S(2)}) async-start(), calls=%async_computation.19 | async-start | bytes 2359296 | tf_op jit(solution)/shard_map/all_gather | solution.py:144
  28.7 273.0 %reduce-scatter.9.cloned.1.call-start = ((), (), s32[]{:S(2)}) async-start(), calls=%async_computation.8 | async-start | bytes 8847360 | tf_op jit(solution)/shard_map/reduce_scatter | solution.py:191
  29.4 96.0 %copy-start.197 = (f32[1,512]{1,0:T(1,128)}, f32[1,512]{1,0:T(1,128)S(1)}, u32[]{:S(2)}) copy-start(f32[1,512]{1,0:T(1,128)S(1)} %get-tuple-element.273) | copy-start | bytes 6148
  29.4 96.0 %copy-start.199 = (f32[1,512]{1,0:T(1,128)}, f32[1,512]{1,0:T(1,128)S(1)}, u32[]{:S(2)}) copy-start(f32[1,512]{1,0:T(1,128)S(1)} %get-tuple-element.274) | copy-start | bytes 6148
  29.4 96.0 %copy-start.201 = (f32[1,512]{1,0:T(1,128)}, f32[1,512]{1,0:T(1,128)S(1)}, u32[]{:S(2)}) copy-start(f32[1,512]{1,0:T(1,128)S(1)} %get-tuple-element.275) | copy-start | bytes 6148
  29.4 96.0 %copy-start.203 = (f32[1,512]{1,0:T(1,128)}, f32[1,512]{1,0:T(1,128)S(1)}, u32[]{:S(2)}) copy-start(f32[1,512]{1,0:T(1,128)S(1)} %get-tuple-element.276) | copy-start | bytes 6148
  30.1 83.3 %copy-start.228 = (f32[8]{0:T(128)}, f32[8]{0:T(128)S(1)}, u32[]{:S(2)}) copy-start(f32[8]{0:T(128)S(1)} %get-tuple-element.265) | copy-start | bytes 100
  30.7 101.1 %copy-start.233 = (f32[1,256]{1,0:T(1,128)}, f32[1,256]{1,0:T(1,128)S(1)}, u32[]{:S(2)}) copy-start(f32[1,256]{1,0:T(1,128)S(1)} %get-tuple-element.283) | copy-start | bytes 3076
  30.7 101.1 %copy-start.235 = (f32[1,256]{1,0:T(1,128)}, f32[1,256]{1,0:T(1,128)S(1)}, u32[]{:S(2)}) copy-start(f32[1,256]{1,0:T(1,128)S(1)} %get-tuple-element.284) | copy-start | bytes 3076
  30.7 101.1 %copy-start.237 = (f32[1,256]{1,0:T(1,128)}, f32[1,256]{1,0:T(1,128)S(1)}, u32[]{:S(2)}) copy-start(f32[1,256]{1,0:T(1,128)S(1)} %get-tuple-element.285) | copy-start | bytes 3076
  30.7 101.1 %copy-start.239 = (f32[1,256]{1,0:T(1,128)}, f32[1,256]{1,0:T(1,128)S(1)}, u32[]{:S(2)}) copy-start(f32[1,256]{1,0:T(1,128)S(1)} %get-tuple-element.286) | copy-start | bytes 3076
  109.7 14.1 %collective-permute-start = (f32[1,3,768]{1,2,0:T(8,128)S(1)}, f32[1,3,768]{1,2,0:T(8,128)S(1)}, u32[]{:S(2)}, u32[]{:S(2)}) collective-permute-start(f32[1,3,768]{1,2,0:T(8,128)S(1)} %concatenate.212), channel_id=1, source_target_pairs={{0,16},{1,17},{2,18},{3,19},{4,20},{5,21},{6,22},{7,23},{8,24},{9,... | collective-permute-start | bytes 27656 | tf_op jit(solution)/shard_map/jvp()/ppermute | solution.py:23
  140.5 9.9 collective-permute-start.1
  176.3 169.7 %all-gather.20.cloned.1.call-start = ((), (), s32[]{:S(2)}) async-start(), calls=%async_computation.20 | async-start | bytes 1966080 | tf_op jit(solution)/shard_map/all_gather | solution.py:183
  308.3 237.4 %reduce-scatter.11.cloned.1.call-start = ((), (), s32[]{:S(2)}) async-start(), calls=%async_computation.9 | async-start | bytes 8847360 | tf_op jit(solution)/shard_map/reduce_scatter | solution.py:191
  352.4 11.6 collective-permute-start.3
  381.6 11.5 collective-permute-start.4
  423.8 169.1 %all-gather.22.cloned.1.call-start = ((), (), s32[]{:S(2)}) async-start(), calls=%async_computation.21 | async-start | bytes 2211840 | tf_op jit(solution)/shard_map/all_gather | solution.py:183
  427.6 122.3 %copy-start.282 = (pred[3]{0:T(512)(128)(4,1)}, pred[3]{0:T(512)(128)(4,1)S(1)}, u32[]{:S(2)}) copy-start(pred[3]{0:T(512)(128)(4,1)S(1)} %compare_or_fusion) | copy-start | bytes 13
  552.0 256.1 %reduce-scatter.13.cloned.1.call-start = ((), (), s32[]{:S(2)}) async-start(), calls=%async_computation.10 | async-start | bytes 7864320 | tf_op jit(solution)/shard_map/reduce_scatter | solution.py:191
  614.0 15.2 %collective-permute-start.6 = (f32[1,8,64,128]{3,2,1,0:T(8,128)}, f32[1,8,64,128]{3,2,1,0:T(8,128)}, u32[]{:S(2)}, u32[]{:S(2)}) collective-permute-start(f32[1,8,64,128]{3,2,1,0:T(8,128)} %get-tuple-element.197), channel_id=1, source_target_pairs={{16,0},{17,1},{18,2},{19,3},{20,4},{21,5},{22,6},{23,7},{24,8},{25... | collective-permute-start | bytes 786440 | tf_op jit(solution)/shard_map/transpose(jvp())/ppermute | solution.py:23
  668.2 13.7 %collective-permute-start.7 = (f32[1,3,768]{1,2,0:T(8,128)}, f32[1,3,768]{1,2,0:T(8,128)}, u32[]{:S(2)}, u32[]{:S(2)}) collective-permute-start(f32[1,3,768]{1,2,0:T(8,128)} %pad_add_fusion.17), channel_id=1, source_target_pairs={{16,0},{17,1},{18,2},{19,3},{20,4},{21,5},{22,6},{23,7},{24,8},{25... | collective-permute-start | bytes 27656 | tf_op jit(solution)/shard_map/transpose(jvp())/ppermute | solution.py:23
  699.0 109.0 %copy-start.176 = (f32[3,64]{1,0:T(4,128)S(1)}, f32[3,64]{1,0:T(4,128)}, u32[]{:S(2)}) copy-start(f32[3,64]{1,0:T(4,128)} %copy-done.175) | copy-start | bytes 2308
  699.1 111.7 %copy-start.174 = (f32[1,3,64,1]{2,1,3,0:T(4,128)S(1)}, f32[1,3,64,1]{2,1,3,0:T(4,128)}, u32[]{:S(2)}) copy-start(f32[1,3,64,1]{2,1,3,0:T(4,128)} %copy-done.173) | copy-start | bytes 2308
  699.1 111.7 %copy-start.255 = (f32[3,64]{1,0:T(4,128)S(1)}, f32[3,64]{1,0:T(4,128)}, u32[]{:S(2)}) copy-start(f32[3,64]{1,0:T(4,128)} %get-tuple-element.304) | copy-start | bytes 2308
  699.1 111.7 %copy-start.283 = (pred[3]{0:T(512)(128)(4,1)S(1)}, pred[3]{0:T(512)(128)(4,1)}, u32[]{:S(2)}) copy-start(pred[3]{0:T(512)(128)(4,1)} %copy-done.282) | copy-start | bytes 13
  699.1 157.2 %all-gather.24.cloned.1.call-start = ((), (), s32[]{:S(2)}) async-start(), calls=%async_computation.22 | async-start | bytes 2211840 | tf_op jit(solution)/shard_map/all_gather | solution.py:183
  815.3 231.0 %reduce-scatter.21.cloned.1.call-start = ((), (), s32[]{:S(2)}) async-start(), calls=%async_computation.14 | async-start | bytes 6594560 | tf_op jit(solution)/shard_map/reduce_scatter | solution.py:250
  821.8 227.1 %reduce-scatter.23.cloned.1.call-start = ((), (), s32[]{:S(2)}) async-start(), calls=%async_computation.15 | async-start | bytes 2621440 | tf_op jit(solution)/shard_map/reduce_scatter | solution.py:242
  826.7 229.4 %reduce-scatter.17.cloned.1.call-start = ((), (), s32[]{:S(2)}) async-start(), calls=%async_computation.12 | async-start | bytes 6594560 | tf_op jit(solution)/shard_map/reduce_scatter | solution.py:250
  877.3 15.1 %collective-permute-start.8 = (f32[1,8,64,128]{3,2,1,0:T(8,128)}, f32[1,8,64,128]{3,2,1,0:T(8,128)}, u32[]{:S(2)}, u32[]{:S(2)}) collective-permute-start(f32[1,8,64,128]{3,2,1,0:T(8,128)} %get-tuple-element.179), channel_id=1, source_target_pairs={{16,0},{17,1},{18,2},{19,3},{20,4},{21,5},{22,6},{23,7},{24,8},{25... | collective-permute-start | bytes 786440 | tf_op jit(solution)/shard_map/transpose(jvp())/ppermute | solution.py:23
  922.1 13.5 %collective-permute-start.9 = (f32[1,3,768]{1,2,0:T(8,128)S(1)}, f32[1,3,768]{1,2,0:T(8,128)S(1)}, u32[]{:S(2)}, u32[]{:S(2)}) collective-permute-start(f32[1,3,768]{1,2,0:T(8,128)S(1)} %pad_add_fusion.16), channel_id=1, source_target_pairs={{16,0},{17,1},{18,2},{19,3},{20,4},{21,5},{22,6},{23,7},{24,8},{25... | collective-permute-start | bytes 27656 | tf_op jit(solution)/shard_map/transpose(jvp())/ppermute | solution.py:23
  942.2 116.4 %reduce-scatter.19.cloned.1.call-start = ((), (), s32[]{:S(2)}) async-start(), calls=%async_computation.13 | async-start | bytes 2621440 | tf_op jit(solution)/shard_map/reduce_scatter | solution.py:242
  947.0 197.8 %reduce-scatter.15.cloned.1.call-start = ((), (), s32[]{:S(2)}) async-start(), calls=%async_computation.11 | async-start | bytes 7864320 | tf_op jit(solution)/shard_map/reduce_scatter | solution.py:191
  964.6 285.4 %all-reduce.109.cloned.1.call-start = ((), (), s32[]{:S(2)}) async-start(), calls=%async_computation.16 | async-start | bytes 524288 | tf_op jit(solution)/shard_map/psum | solution.py:292
  965.0 15.3 %collective-permute-start.2 = (f32[1,2,64,1024]{3,2,1,0:T(8,128)S(1)}, f32[1,2,64,1024]{3,2,1,0:T(8,128)}, u32[]{:S(2)}, u32[]{:S(2)}) collective-permute-start(f32[1,2,64,1024]{3,2,1,0:T(8,128)S(1)} %copy.404), channel_id=1, source_target_pairs={{16,0},{17,1},{18,2},{19,3},{20,4},{21,5},{22,6},{23,7},{24,8},{25... | collective-permute-start | bytes 1572872 | tf_op jit(solution)/shard_map/ppermute | solution.py:23
  969.1 21.7 %collective-permute-start.5 = (f32[1,3,64,1024]{3,2,1,0:T(8,128)}, f32[1,3,64,1024]{3,2,1,0:T(8,128)}, u32[]{:S(2)}, u32[]{:S(2)}) collective-permute-start(f32[1,3,64,1024]{3,2,1,0:T(8,128)} %copy.419), channel_id=1, source_target_pairs={{0,16},{1,17},{2,18},{3,19},{4,20},{5,21},{6,22},{7,23},{8,24},{9,... | collective-permute-start | bytes 2359304 | tf_op jit(solution)/shard_map/ppermute | solution.py:23
  996.3 19.9 %collective-permute-start.11 = (f32[1,3,64,1024]{3,2,1,0:T(8,128)}, f32[1,3,64,1024]{3,2,1,0:T(8,128)}, u32[]{:S(2)}, u32[]{:S(2)}) collective-permute-start(f32[1,3,64,1024]{3,2,1,0:T(8,128)} %copy.464), channel_id=1, source_target_pairs={{0,16},{1,17},{2,18},{3,19},{4,20},{5,21},{6,22},{7,23},{8,24},{9,... | collective-permute-start | bytes 2359304 | tf_op jit(solution)/shard_map/ppermute | solution.py:23
  1050.7 94.1 %copy-start.12 = (bf16[1,3,64,1024]{2,3,1,0:T(8,128)(2,1)S(1)}, bf16[1,3,64,1024]{2,3,1,0:T(8,128)(2,1)}, u32[]{:S(2)}) copy-start(bf16[1,3,64,1024]{2,3,1,0:T(8,128)(2,1)} %copy-done.11) | copy-start | bytes 1179652
  1050.7 94.1 %copy-start.160 = (f32[1,1024]{1,0:T(1,128)S(1)}, f32[1,1024]{1,0:T(1,128)}, u32[]{:S(2)}) copy-start(f32[1,1024]{1,0:T(1,128)} %copy-done.159) | copy-start | bytes 12292
  1050.7 94.1 %copy-start.167 = (f32[3,64]{1,0:T(4,128)S(1)}, f32[3,64]{1,0:T(4,128)}, u32[]{:S(2)}) copy-start(f32[3,64]{1,0:T(4,128)} %copy-done.166) | copy-start | bytes 2308
  1050.7 160.2 %collective-permute-start.13 = (f32[256,1800]{0,1:T(8,128)}, f32[256,1800]{0,1:T(8,128)}, u32[]{:S(2)}, u32[]{:S(2)}) collective-permute-start(f32[256,1800]{0,1:T(8,128)} %constant_dynamic-update-slice_fusion.3), channel_id=1, source_target_pairs={{0,16},{1,17},{2,18},{3,19},{4,20},{5,21},{6,22},{7,23},{8,24},{9,... | collective-permute-start | bytes 5529608 | tf_op jit(solution)/shard_map/ppermute | solution.py:23
  1058.6 88.4 %copy-start.249 = (f32[3,64]{1,0:T(4,128)S(1)}, f32[3,64]{1,0:T(4,128)}, u32[]{:S(2)}) copy-start(f32[3,64]{1,0:T(4,128)} %get-tuple-element.302) | copy-start | bytes 2308
  1060.5 150.5 %collective-permute-start.12 = (f32[256,1800]{0,1:T(8,128)}, f32[256,1800]{0,1:T(8,128)}, u32[]{:S(2)}, u32[]{:S(2)}) collective-permute-start(f32[256,1800]{0,1:T(8,128)} %constant_dynamic-update-slice_fusion.1), channel_id=1, source_target_pairs={{16,0},{17,1},{18,2},{19,3},{20,4},{21,5},{22,6},{23,7},{24,8},{25... | collective-permute-start | bytes 5529608 | tf_op jit(solution)/shard_map/ppermute | solution.py:23
  1151.4 50.8 %collective-permute-start.10 = (f32[1,2,64,1024]{3,2,1,0:T(8,128)S(1)}, f32[1,2,64,1024]{3,2,1,0:T(8,128)}, u32[]{:S(2)}, u32[]{:S(2)}) collective-permute-start(f32[1,2,64,1024]{3,2,1,0:T(8,128)S(1)} %copy.462), channel_id=1, source_target_pairs={{16,0},{17,1},{18,2},{19,3},{20,4},{21,5},{22,6},{23,7},{24,8},{25... | collective-permute-start | bytes 1572872 | tf_op jit(solution)/shard_map/ppermute | solution.py:23
  (293 other events, 1392.5 us)
Sparse Core Ops, SparseCore 0:
  24.6 37.2 all-gather.13
  64.4 41.0 all-gather.15
  108.0 30.8 all-gather.17
  176.4 125.2 reduce-scatter.8
  308.4 37.5 all-gather.19
  424.0 121.6 reduce-scatter.10
  552.1 40.8 all-gather.21
  699.2 108.8 reduce-scatter.12
  815.4 40.8 all-gather.23
  858.7 50.4 reduce-scatter.20
  911.9 31.4 reduce-scatter.22
  945.8 51.6 reduce-scatter.16
  1000.1 31.6 reduce-scatter.18
  1034.0 110.7 reduce-scatter.14
  1215.5 34.4 all-reduce.108

commit v2 on v1

--- a/solution.py
+++ b/solution.py
@@ -15,12 +15,41 @@
 EPSILON = 1e-05
 EXACT = lax.Precision.HIGHEST
 FULL_PRECISION = lax.Precision.HIGH
-LINK = jnp.float32
+LINK = jnp.bfloat16
 
 
 def shifted(block, distance):
     route = [(0, 1)] if distance == 1 else [(1, 0)]
     return lax.ppermute(block, "section", route)
+
+
+def swapped(block):
+    return lax.ppermute(block, "section", [(0, 1), (1, 0)])
+
+
+def in_order(values, axis):
+    count = lax.axis_size(axis)
+    me = lax.axis_index(axis)
+    whole = jnp.zeros((count,) + values.shape, values.dtype)
+    for step in range(count):
+        route = [(i, (i + step) % count) for i in range(count)]
+        part = lax.ppermute(values, axis, route) if step else values
+        whole = lax.dynamic_update_index_in_dim(whole, part, lax.rem(me + count - step, count), 0)
+    return whole
+
+
+def sum_for_owner(term_for, axis, link):
+    count = lax.axis_size(axis)
+    me = lax.axis_index(axis)
+    arrived = []
+    for step in range(1, count):
+        route = [(i, (i + step) % count) for i in range(count)]
+        term = term_for(lax.rem(me + step, count)).astype(link)
+        arrived.append(lax.ppermute(term, axis, route))
+    summed = term_for(me)
+    for term in arrived:
+        summed = summed + term.astype(jnp.float32)
+    return summed
 
 
 def causal_conv(padded, tap_rows):
@@ -149,19 +178,19 @@
     )
     out_local = lax.dynamic_slice_in_dim(out_weight[0], tensor_rank * width, width, 0)
     out_weights_t = both_layers(out_local.T)
-    small_in = lax.all_gather(
-        jnp.concatenate(
-            [
-                norm_gain[0],
-                lax.dynamic_slice_in_dim(gate_gain[0], tensor_rank * width, width, 0),
-                conv_inner[0].reshape(-1),
-                conv_state[0].reshape(-1),
-                head_params[0].reshape(-1),
-            ]
-        ),
-        "section",
-        axis=0,
-        tiled=False,
+    own_small = jnp.concatenate(
+        [
+            norm_gain[0],
+            lax.dynamic_slice_in_dim(gate_gain[0], tensor_rank * width, width, 0),
+            conv_inner[0].reshape(-1),
+            conv_state[0].reshape(-1),
+            head_params[0].reshape(-1),
+        ]
+    )
+    other_small = swapped(own_small)
+    small_in = (
+        jnp.where(first_section, own_small, other_small),
+        jnp.where(first_section, other_small, own_small),
     )
 
     def split_small(vector):
@@ -180,17 +209,35 @@
         return parts
 
     def spread_rows(values):
-        gathered = lax.all_gather(values, "tensor", axis=0, tiled=False)
-        return jnp.transpose(gathered, (1, 2, 0, 3, 4)).reshape(seqs, rows, values.shape[-1])
-
-    def by_rank(values):
+        columns = values.shape[-1]
+        whole = jnp.zeros((seqs, held_blocks, ranks, part_rows, columns), values.dtype)
+        for step in range(ranks):
+            route = [(i, (i + step) % ranks) for i in range(ranks)]
+            part = lax.ppermute(values, "tensor", route) if step else values
+            source = lax.rem(tensor_rank + ranks - step, ranks)
+            whole = lax.dynamic_update_slice_in_dim(whole, part[:, :, None], source, 2)
+        return whole.reshape(seqs, rows, columns)
+
+    def rows_of(values, rank):
         split = values.reshape(seqs, held_blocks, ranks, part_rows, values.shape[-1])
-        return jnp.transpose(split, (2, 0, 1, 3, 4))
-
-    def row_sums(partial):
-        return lax.psum_scatter(
-            partial.astype(LINK), "tensor", scatter_dimension=0, tiled=False
-        ).astype(jnp.float32)
+        return lax.dynamic_index_in_dim(split, rank, 2, keepdims=False)
+
+    def row_sums(values, weights):
+        def term_for(rank):
+            return jnp.einsum(
+                "bgqc,dc->bgqd", rows_of(values, rank), weights, preferred_element_type=jnp.float32
+            )
+
+        return sum_for_owner(term_for, "tensor", LINK)
+
+    shard = gate_weight.shape[1]
+
+    def weight_sums(left, right):
+        def term_for(rank):
+            part = lax.dynamic_slice_in_dim(left, rank * shard, shard, 2)
+            return jnp.einsum("btd,btc->dc", part, right, preferred_element_type=jnp.float32)
+
+        return sum_for_owner(term_for, "dp", LINK)
 
     def forward(hidden, layer):
         gain_rows, gate_scale, taps_inner, taps_state, head_rows = split_small(small_in[layer])
@@ -209,14 +256,12 @@
             head_rows,
         )
         scaled = (gate_out * gate_scale).astype(jnp.bfloat16)
-        partial = jnp.einsum(
-            "kbgqc,dc->kbgqd", by_rank(scaled), out_t, preferred_element_type=jnp.float32
-        )
-        squares = by_rank(jnp.sum(gate_out * gate_out, axis=2, keepdims=True))
-        squares = jnp.pad(squares, ((0, 0),) * 4 + ((0, SIDE - 1),))
-        summed = row_sums(jnp.concatenate([partial, squares], 4))
-        inv_gate = lax.rsqrt(summed[..., D : D + 1] / INNER + EPSILON)
-        branch = inv_gate * summed[..., :D]
+        squares = jnp.sum(gate_out * gate_out, axis=2, keepdims=True)
+        squares = sum_for_owner(
+            lambda rank: rows_of(squares, rank)[..., 0], "tensor", jnp.float32
+        )
+        inv_gate = lax.rsqrt(squares / INNER + EPSILON)[..., None]
+        branch = inv_gate * row_sums(scaled, out_t)
         kept = (hidden, inv_rms, normed, pullback, gate_out, scaled, inv_gate, branch)
         return hidden + branch, kept
 
@@ -238,16 +283,12 @@
             jnp.float32
         )
         through = jnp.einsum("btd,dc->btc", upper, out_t, preferred_element_type=jnp.float32)
-        out_grad = jnp.einsum("btd,btc->dc", upper, scaled, preferred_element_type=jnp.float32)
-        out_grad = lax.psum_scatter(out_grad, "dp", scatter_dimension=0, tiled=True)
+        out_grad = weight_sums(upper, scaled)
         gate_gain_grad = jnp.sum(through * gate_out, axis=(0, 1))
         parts = pullback(gate_scale * through - gate_out * pull_full)
         low = jnp.concatenate([part.astype(jnp.bfloat16) for part in parts[:4]], 2)
-        grad_normed = row_sums(
-            jnp.einsum("kbgqc,dc->kbgqd", by_rank(low), proj, preferred_element_type=jnp.float32)
-        )
-        proj_grad = jnp.einsum("btd,btc->dc", normed, low, preferred_element_type=jnp.float32)
-        proj_grad = lax.psum_scatter(proj_grad, "dp", scatter_dimension=0, tiled=True)
+        grad_normed = row_sums(low, proj)
+        proj_grad = weight_sums(normed, low)
         norm_gain_grad = jnp.sum(grad_normed * hidden * inv_rms, axis=(0, 1, 2))
         inner_in = jnp.sum(grad_normed * gain_rows * hidden, axis=3, keepdims=True)
         grad_in = grad_out + inv_rms * gain_rows * grad_normed - hidden * inv_rms**3 * inner_in / D
@@ -276,10 +317,10 @@
 
     top_grad = jnp.where(block_valid, held(cotangent), 0.0)
     grad_second, weights_second, shared_second, own_second = backward(top_grad, 1, kept_second)
-    weights_to_second = shifted(weights_second, 1)
+    weights_to_second = shifted(weights_second.astype(LINK), 1).astype(jnp.float32)
     grad_to_second = shifted(grad_second, 1)
     grad_first, weights_first, shared_first, own_first = backward(grad_second, 0, kept_first)
-    weights_to_first = shifted(weights_first, -1)
+    weights_to_first = shifted(weights_first.astype(LINK), -1).astype(jnp.float32)
     input_grad = joined(
         grad_first, grad_second, shifted(grad_first[:, extra:], -1), grad_to_second
     )
@@ -289,11 +330,19 @@
     state_at = 2 * width
     step_at = state_at + 2 * STATE
     out_at = step_at + heads_loc
-    state_grad = lax.psum(weights[:, state_at:step_at], "tensor")
-    shared = lax.psum(jnp.stack([shared_first, shared_second]), ("section", "dp", "tensor"))
-    own = lax.psum(jnp.stack([own_first, own_second]), ("section", "dp"))
-    shared = jnp.where(first_section, shared[0], shared[1])
-    own = jnp.where(first_section, own[0], own[1])
+    small_first = jnp.sum(in_order(jnp.concatenate([shared_first, own_first]), "dp"), axis=0)
+    small_second = jnp.sum(in_order(jnp.concatenate([shared_second, own_second]), "dp"), axis=0)
+    small = jnp.where(first_section, small_first, small_second) + swapped(
+        jnp.where(first_section, small_second, small_first)
+    )
+    shared_count = shared_first.shape[0]
+    own = small[shared_count:]
+    over_heads = jnp.concatenate(
+        [weights[:, state_at:step_at].reshape(-1), small[:shared_count]]
+    ).astype(LINK)
+    over_heads = jnp.sum(in_order(over_heads, "tensor").astype(jnp.float32), axis=0)
+    state_grad = over_heads[:-shared_count].reshape(shard, 2 * STATE)
+    shared = over_heads[-shared_count:]
     taps_end = width * (CONV + 2)
     return (
         output[None],

time: 1270 us -> 829 us (0.65)
  waiting for transfers between devices: 690 us -> 223 us
  starting transfers between devices: 43.2 us -> 158 us
  blocking collectives: 81.3 us -> 0 us
  local copies, waits for them, and re-layouts: 171 us -> 148 us
  matrix products: 129 us -> 149 us
    reduce_scatter x8 -> x0, waiting for transfers between devices: 435 us -> none  [the longest x4 435 us: row_sums(): lax.psum_scatter(partial.astype(LINK), 'tensor', scatter_dimension=0, til...]
    ppermute x0 -> x53, waiting for transfers between devices: none -> 184 us  [the longest x12 83.9 us: spread_rows(): part = lax.ppermute(values, 'tensor', route) if step else values]
    all_gather x4 -> x0, waiting for transfers between devices: 138 us -> none  [spread_rows(): gathered = lax.all_gather(values, 'tensor', axis=0, tiled=False)]
    ppermute x0 -> x53, starting transfers between devices: none -> 121 us  [the longest x30 60.7 us: sum_for_owner(): arrived.append(lax.ppermute(term, axis, route))]
    psum x2 -> x0, blocking collectives: 71.2 us -> none  [the longest x1 48.2 us: per_device(): lax.psum(jnp.stack([shared_first, shared_second]), ('section', 'dp', 'ten...]
    all_gather x2, waiting for transfers between devices: 41.9 us -> 8.17 us  [both_layers(): gathered = lax.all_gather(values, ('section', 'dp'), axis=0, tiled=False)]
    psum x1 -> x0, waiting for transfers between devices: 28.8 us -> none  [per_device(): state_grad = lax.psum(weights[:, state_at:step_at], 'tensor')]
    dynamic_update_slice x0 -> x24, local copies, waits for them, and re-layouts: none -> 26.2 us  [the longest x12 25.8 us: in_order(): lax.dynamic_update_index_in_dim(whole, part, lax.rem(me + count - step, c...]
  transfers between devices with their start and end apart: 29 -> 69, of which waited for: 18 -> 24; matrix products, arithmetic and copies ran while one was open for 19% -> 39% of each run, Pallas kernels for 0% -> 0%
where the time goes in v2:
time: 829 us; the launch traced here: 818 us
  waiting for transfers between devices  223 us (27%)
  starting transfers between devices  158 us (19%)
  matrix products  149 us (18%)
  local copies, waits for them, and re-layouts  148 us (18%)
  other arithmetic  121 us (15%)
  between operations  19.4 us (2%)
    ppermute x12, waiting for transfers between devices, spread_rows(): part = lax.ppermute(values, 'tensor', route) if step else values  83.9 us
    ppermute x30, waiting for transfers between devices, sum_for_owner(): arrived.append(lax.ppermute(term, axis, route))  75.8 us
    ppermute x30, starting transfers between devices, sum_for_owner(): arrived.append(lax.ppermute(term, axis, route))  60.7 us
    ppermute x12, starting transfers between devices, spread_rows(): part = lax.ppermute(values, 'tensor', route) if step else values  39.4 us
    ppermute x14, starting transfers between devices, shifted(): return lax.ppermute(block, 'section', route)  37 us
    dot_general x16, matrix products, term_for(): jnp.einsum('bgqc,dc->bgqd', rows_of(values, rank), weights, preferred_ele...  37 us
    ppermute x14, waiting for transfers between devices, shifted(): return lax.ppermute(block, 'section', route)  30.4 us
    dot_general x16, matrix products, term_for(): jnp.einsum('btd,btc->dc', part, right, preferred_element_type=jnp.float32)  28.1 us
  transfers between devices with their start and end apart: 69, of which 24 were waited for; matrix products, arithmetic and copies ran while one was open for 39% of the time, Pallas kernels for 0%

profile of v2, /device:TPU:0, one launch (start us, length us, event | category | flops | bytes accessed | tf_op | source)
XLA Modules:
  0.0 817.7 jit_solution(13399702927858455631)
XLA Ops:
  26.4 7.2 collective-permute-done.1
  33.6 15.4 %collective-permute-done.2 = bf16[1,3,64,1024]{3,2,1,0:T(8,128)(2,1)S(1)} collective-permute-done((bf16[1,3,64,1024]{3,2,1,0:T(8,128)(2,1)S(1)}, bf16[1,3,64,1024]{3,2,1,0:T(8,128)(2,1)S(1)}, u32[]{:S(2)}, u32[]{:S(2)}) %collective-permute-start.2) | collective-permute-done | bytes 393248 | tf_op jit(solution)/shard_map/ppermute | solution.py:216
  49.1 8.1 all-gather.5.cloned.1.call-done
  57.3 4.0 convolution_bitcast_fusion.1
  67.7 9.4 %collective-permute-done.4 = f32[1,3,768]{1,2,0:T(8,128)S(1)} collective-permute-done((f32[1,3,768]{1,2,0:T(8,128)S(1)}, f32[1,3,768]{1,2,0:T(8,128)S(1)}, u32[]{:S(2)}, u32[]{:S(2)}) %collective-permute-start.4) | collective-permute-done | bytes 9248 | tf_op jit(solution)/shard_map/jvp()/ppermute | solution.py:23
  90.9 4.8 collective-permute-start.5
  113.1 3.7 multiply_reduce_fusion.17
  133.5 19.2 %collective-permute-done.10 = bf16[1,3,64,1024]{3,2,1,0:T(8,128)(2,1)S(1)} collective-permute-done((bf16[1,3,64,1024]{3,2,1,0:T(8,128)(2,1)S(1)}, bf16[1,3,64,1024]{3,2,1,0:T(8,128)(2,1)S(1)}, u32[]{:S(2)}, u32[]{:S(2)}) %collective-permute-start.10) | collective-permute-done | bytes 393248 | tf_op jit(solution)/shard_map/ppermute | solution.py:48
  157.9 14.9 %collective-permute-start.13 = (bf16[1,3,64,1024]{3,2,1,0:T(8,128)(2,1)S(1)}, bf16[1,3,64,1024]{3,2,1,0:T(8,128)(2,1)S(1)}, u32[]{:S(2)}, u32[]{:S(2)}) collective-permute-start(bf16[1,3,64,1024]{3,2,1,0:T(8,128)(2,1)S(1)} %get-tuple-element.214), channel_id=1, source_target_pairs={{0,1},{1,2},{2,3},{3,0},{4,5},{5,6},{6,7},{7,4},{8,9},{9,10},{10,1... | collective-permute-start | bytes 1179656 | tf_op jit(solution)/shard_map/ppermute | solution.py:216
  176.1 6.2 collective-permute-done.13
  182.4 10.5 %collective-permute-done.14 = bf16[1,3,64,1024]{3,2,1,0:T(8,128)(2,1)S(1)} collective-permute-done((bf16[1,3,64,1024]{3,2,1,0:T(8,128)(2,1)S(1)}, bf16[1,3,64,1024]{3,2,1,0:T(8,128)(2,1)S(1)}, u32[]{:S(2)}, u32[]{:S(2)}) %collective-permute-start.14) | collective-permute-done | bytes 393248 | tf_op jit(solution)/shard_map/ppermute | solution.py:216
  192.9 5.4 collective-permute-done.15
  200.8 4.3 collective-permute-start.16
  230.9 5.3 collective-permute-start.17
  271.2 9.0 %collective-permute-start.21 = (bf16[1,3,64,1024]{3,2,1,0:T(8,128)(2,1)}, bf16[1,3,64,1024]{3,2,1,0:T(8,128)(2,1)}, u32[]{:S(2)}, u32[]{:S(2)}) collective-permute-start(bf16[1,3,64,1024]{3,2,1,0:T(8,128)(2,1)} %fusion.177), channel_id=1, source_target_pairs={{0,1},{1,2},{2,3},{3,0},{4,5},{5,6},{6,7},{7,4},{8,9},{9,10},{10,1... | collective-permute-start | bytes 1179656 | tf_op jit(solution)/shard_map/ppermute | solution.py:48
  292.6 15.1 %collective-permute-done.18 = f32[1,3,64]{2,0,1:T(1,128)} collective-permute-done((f32[1,3,64]{2,0,1:T(1,128)}, f32[1,3,64]{2,0,1:T(1,128)}, u32[]{:S(2)}, u32[]{:S(2)}) %collective-permute-start.18) | collective-permute-done | bytes 800 | tf_op jit(solution)/shard_map/ppermute | solution.py:48
  309.7 6.5 collective-permute-done.19
  318.3 3.6 multiply_convert_fusion.3
  329.2 6.5 collective-permute-start.24
  340.2 17.5 %collective-permute-done.26 = bf16[1,3,64,1152]{3,2,1,0:T(8,128)(2,1)S(1)} collective-permute-done((bf16[1,3,64,1152]{3,2,1,0:T(8,128)(2,1)S(1)}, bf16[1,3,64,1152]{3,2,1,0:T(8,128)(2,1)S(1)}, u32[]{:S(2)}, u32[]{:S(2)}) %collective-permute-start.26) | collective-permute-done | bytes 442400 | tf_op jit(solution)/shard_map/ppermute | solution.py:216
  358.2 6.1 multiply_reduce_fusion.4
  372.3 3.5 fusion.203
  381.1 6.2 fusion.41
  421.4 4.7 multiply_reduce_fusion.8
  453.4 8.4 %collective-permute-done.29 = f32[1,3,768]{1,2,0:T(8,128)S(1)} collective-permute-done((f32[1,3,768]{1,2,0:T(8,128)}, f32[1,3,768]{1,2,0:T(8,128)S(1)}, u32[]{:S(2)}, u32[]{:S(2)}) %collective-permute-start.29) | collective-permute-done | bytes 9248 | tf_op jit(solution)/shard_map/transpose(jvp())/ppermute | solution.py:23
  465.5 4.2 copy.489
  472.6 9.2 %collective-permute-start.30 = (bf16[1,3,64,1024]{3,2,1,0:T(8,128)(2,1)S(1)}, bf16[1,3,64,1024]{3,2,1,0:T(8,128)(2,1)S(1)}, u32[]{:S(2)}, u32[]{:S(2)}) collective-permute-start(bf16[1,3,64,1024]{3,2,1,0:T(8,128)(2,1)S(1)} %fusion.195), channel_id=1, source_target_pairs={{0,1},{1,2},{2,3},{3,0},{4,5},{5,6},{6,7},{7,4},{8,9},{9,10},{10,1... | collective-permute-start | bytes 1179656 | tf_op jit(solution)/shard_map/ppermute | solution.py:48
  498.7 7.1 collective-permute-done.31
  508.8 8.9 %collective-permute-start.33 = (bf16[1,3,64,1152]{3,2,1,0:T(8,128)(2,1)S(1)}, bf16[1,3,64,1152]{3,2,1,0:T(8,128)(2,1)S(1)}, u32[]{:S(2)}, u32[]{:S(2)}) collective-permute-start(bf16[1,3,64,1152]{3,2,1,0:T(8,128)(2,1)S(1)} %fusion.328), channel_id=1, source_target_pairs={{0,1},{1,2},{2,3},{3,0},{4,5},{5,6},{6,7},{7,4},{8,9},{9,10},{10,1... | collective-permute-start | bytes 1327112 | tf_op jit(solution)/shard_map/ppermute | solution.py:216
  531.5 16.0 %collective-permute-done.34 = bf16[1,3,64,1152]{3,2,1,0:T(8,128)(2,1)S(1)} collective-permute-done((bf16[1,3,64,1152]{3,2,1,0:T(8,128)(2,1)S(1)}, bf16[1,3,64,1152]{3,2,1,0:T(8,128)(2,1)S(1)}, u32[]{:S(2)}, u32[]{:S(2)}) %collective-permute-start.34) | collective-permute-done | bytes 442400 | tf_op jit(solution)/shard_map/ppermute | solution.py:216
  547.9 5.3 multiply_reduce_fusion.9
  568.2 6.2 fusion.43
  593.4 3.9 fusion.60
  615.7 4.1 fusion.54
  624.9 3.9 multiply_reduce_fusion.13
  638.5 7.6 collective-permute-done.37
  654.5 3.6 fusion.186
  658.1 9.9 %collective-permute-start.38 = (bf16[1,3,64,1024]{3,2,1,0:T(8,128)(2,1)}, bf16[1,3,64,1024]{3,2,1,0:T(8,128)(2,1)}, u32[]{:S(2)}, u32[]{:S(2)}) collective-permute-start(bf16[1,3,64,1024]{3,2,1,0:T(8,128)(2,1)} %fusion.186), channel_id=1, source_target_pairs={{0,1},{1,2},{2,3},{3,0},{4,5},{5,6},{6,7},{7,4},{8,9},{9,10},{10,1... | collective-permute-start | bytes 1179656 | tf_op jit(solution)/shard_map/ppermute | solution.py:48
  689.2 6.7 collective-permute-done.39
  700.8 13.0 %collective-permute-done.44 = bf16[256,1288]{0,1:T(8,128)(2,1)S(1)} collective-permute-done((bf16[256,1288]{0,1:T(8,128)(2,1)}, bf16[256,1288]{0,1:T(8,128)(2,1)S(1)}, u32[]{:S(2)}, u32[]{:S(2)}) %collective-permute-start.44) | collective-permute-done | bytes 659488 | tf_op jit(solution)/shard_map/ppermute | solution.py:48
  714.7 5.7 collective-permute-done.45
  729.7 4.4 collective-permute-start.63
  734.2 24.4 %collective-permute-done.63 = f32[5400]{0:T(1024)S(1)} collective-permute-done((f32[5400]{0:T(1024)S(1)}, f32[5400]{0:T(1024)S(1)}, u32[]{:S(2)}, u32[]{:S(2)}) %collective-permute-start.63) | collective-permute-done | bytes 21632 | tf_op jit(solution)/shard_map/ppermute | solution.py:27
  766.7 6.3 collective-permute-start.64
  780.8 5.8 dynamic_update_slice.110
  787.3 5.8 dynamic_update_slice.111
  794.3 5.8 dynamic_update_slice.112
  801.1 5.8 dynamic_update_slice.113
  (1180 shorter events, 419.0 us)
Async XLA Ops:
  7.2 50.0 %all-gather.5.cloned.1.call-start = ((), (), s32[]{:S(2)}) async-start(), calls=%async_computation | async-start | bytes 5935104 | tf_op jit(solution)/shard_map/all_gather | solution.py:173
  12.2 111.9 %all-gather.7.cloned.1.call-start = ((), (), s32[]{:S(2)}) async-start(), calls=%async_computation.1 | async-start | bytes 2359296 | tf_op jit(solution)/shard_map/all_gather | solution.py:173
  21.2 27.8 %collective-permute-start.2 = (bf16[1,3,64,1024]{3,2,1,0:T(8,128)(2,1)S(1)}, bf16[1,3,64,1024]{3,2,1,0:T(8,128)(2,1)S(1)}, u32[]{:S(2)}, u32[]{:S(2)}) collective-permute-start(bf16[1,3,64,1024]{3,2,1,0:T(8,128)(2,1)S(1)} %get-tuple-element.229), channel_id=1, source_target_pairs={{0,2},{1,3},{2,0},{3,1},{4,6},{5,7},{6,4},{7,5},{8,10},{9,11},{10,... | collective-permute-start | bytes 1179656 | tf_op jit(solution)/shard_map/ppermute | solution.py:216
  23.8 25.3 %collective-permute-start.3 = (bf16[1,3,64,1024]{3,2,1,0:T(8,128)(2,1)S(1)}, bf16[1,3,64,1024]{3,2,1,0:T(8,128)(2,1)S(1)}, u32[]{:S(2)}, u32[]{:S(2)}) collective-permute-start(bf16[1,3,64,1024]{3,2,1,0:T(8,128)(2,1)S(1)} %get-tuple-element.229), channel_id=1, source_target_pairs={{0,3},{1,0},{2,1},{3,2},{4,7},{5,4},{6,5},{7,6},{8,11},{9,8},{10,9... | collective-permute-start | bytes 1179656 | tf_op jit(solution)/shard_map/ppermute | solution.py:216
  126.1 26.7 %collective-permute-start.10 = (bf16[1,3,64,1024]{3,2,1,0:T(8,128)(2,1)S(1)}, bf16[1,3,64,1024]{3,2,1,0:T(8,128)(2,1)S(1)}, u32[]{:S(2)}, u32[]{:S(2)}) collective-permute-start(bf16[1,3,64,1024]{3,2,1,0:T(8,128)(2,1)S(1)} %fusion.175), channel_id=1, source_target_pairs={{0,2},{1,3},{2,0},{3,1},{4,6},{5,7},{6,4},{7,5},{8,10},{9,11},{10,... | collective-permute-start | bytes 1179656 | tf_op jit(solution)/shard_map/ppermute | solution.py:48
  128.4 24.4 %collective-permute-start.9 = (bf16[1,3,64,1024]{3,2,1,0:T(8,128)(2,1)S(1)}, bf16[1,3,64,1024]{3,2,1,0:T(8,128)(2,1)S(1)}, u32[]{:S(2)}, u32[]{:S(2)}) collective-permute-start(bf16[1,3,64,1024]{3,2,1,0:T(8,128)(2,1)S(1)} %fusion.174), channel_id=1, source_target_pairs={{0,1},{1,2},{2,3},{3,0},{4,5},{5,6},{6,7},{7,4},{8,9},{9,10},{10,1... | collective-permute-start | bytes 1179656 | tf_op jit(solution)/shard_map/ppermute | solution.py:48
  129.5 25.6 %collective-permute-start.11 = (bf16[1,3,64,1024]{3,2,1,0:T(8,128)(2,1)S(1)}, bf16[1,3,64,1024]{3,2,1,0:T(8,128)(2,1)S(1)}, u32[]{:S(2)}, u32[]{:S(2)}) collective-permute-start(bf16[1,3,64,1024]{3,2,1,0:T(8,128)(2,1)S(1)} %fusion.176), channel_id=1, source_target_pairs={{0,3},{1,0},{2,1},{3,2},{4,7},{5,4},{6,5},{7,6},{8,11},{9,8},{10,9... | collective-permute-start | bytes 1179656 | tf_op jit(solution)/shard_map/ppermute | solution.py:48
  157.9 24.4 %collective-permute-start.13 = (bf16[1,3,64,1024]{3,2,1,0:T(8,128)(2,1)S(1)}, bf16[1,3,64,1024]{3,2,1,0:T(8,128)(2,1)S(1)}, u32[]{:S(2)}, u32[]{:S(2)}) collective-permute-start(bf16[1,3,64,1024]{3,2,1,0:T(8,128)(2,1)S(1)} %get-tuple-element.214), channel_id=1, source_target_pairs={{0,1},{1,2},{2,3},{3,0},{4,5},{5,6},{6,7},{7,4},{8,9},{9,10},{10,1... | collective-permute-start | bytes 1179656 | tf_op jit(solution)/shard_map/ppermute | solution.py:216
  173.6 24.6 %collective-permute-start.15 = (bf16[1,3,64,1024]{3,2,1,0:T(8,128)(2,1)S(1)}, bf16[1,3,64,1024]{3,2,1,0:T(8,128)(2,1)S(1)}, u32[]{:S(2)}, u32[]{:S(2)}) collective-permute-start(bf16[1,3,64,1024]{3,2,1,0:T(8,128)(2,1)S(1)} %get-tuple-element.214), channel_id=1, source_target_pairs={{0,3},{1,0},{2,1},{3,2},{4,7},{5,4},{6,5},{7,6},{8,11},{9,8},{10,9... | collective-permute-start | bytes 1179656 | tf_op jit(solution)/shard_map/ppermute | solution.py:216
  271.2 47.1 %collective-permute-start.21 = (bf16[1,3,64,1024]{3,2,1,0:T(8,128)(2,1)}, bf16[1,3,64,1024]{3,2,1,0:T(8,128)(2,1)}, u32[]{:S(2)}, u32[]{:S(2)}) collective-permute-start(bf16[1,3,64,1024]{3,2,1,0:T(8,128)(2,1)} %fusion.177), channel_id=1, source_target_pairs={{0,1},{1,2},{2,3},{3,0},{4,5},{5,6},{6,7},{7,4},{8,9},{9,10},{10,1... | collective-permute-start | bytes 1179656 | tf_op jit(solution)/shard_map/ppermute | solution.py:48
  282.7 35.6 %collective-permute-start.22 = (bf16[1,3,64,1024]{3,2,1,0:T(8,128)(2,1)}, bf16[1,3,64,1024]{3,2,1,0:T(8,128)(2,1)}, u32[]{:S(2)}, u32[]{:S(2)}) collective-permute-start(bf16[1,3,64,1024]{3,2,1,0:T(8,128)(2,1)} %fusion.178), channel_id=1, source_target_pairs={{0,2},{1,3},{2,0},{3,1},{4,6},{5,7},{6,4},{7,5},{8,10},{9,11},{10,... | collective-permute-start | bytes 1179656 | tf_op jit(solution)/shard_map/ppermute | solution.py:48
  287.3 31.0 %collective-permute-start.23 = (bf16[1,3,64,1024]{3,2,1,0:T(8,128)(2,1)}, bf16[1,3,64,1024]{3,2,1,0:T(8,128)(2,1)}, u32[]{:S(2)}, u32[]{:S(2)}) collective-permute-start(bf16[1,3,64,1024]{3,2,1,0:T(8,128)(2,1)} %fusion.179), channel_id=1, source_target_pairs={{0,3},{1,0},{2,1},{3,2},{4,7},{5,4},{6,5},{7,6},{8,11},{9,8},{10,9... | collective-permute-start | bytes 1179656 | tf_op jit(solution)/shard_map/ppermute | solution.py:48
  292.6 23.6 %collective-permute-start.19 = (f32[1,3,64]{2,0,1:T(1,128)}, f32[1,3,64]{2,0,1:T(1,128)}, u32[]{:S(2)}, u32[]{:S(2)}) collective-permute-start(f32[1,3,64]{2,0,1:T(1,128)} %get-tuple-element.294), channel_id=1, source_target_pairs={{0,2},{1,3},{2,0},{3,1},{4,6},{5,7},{6,4},{7,5},{8,10},{9,11},{10,... | collective-permute-start | bytes 2312 | tf_op jit(solution)/shard_map/ppermute | solution.py:48
  316.2 177.0 %collective-permute-start.12 = (f32[1,2,64,1024]{3,2,1,0:T(8,128)}, f32[1,2,64,1024]{3,2,1,0:T(8,128)}, u32[]{:S(2)}, u32[]{:S(2)}) collective-permute-start(f32[1,2,64,1024]{3,2,1,0:T(8,128)} %slice.650), channel_id=1, source_target_pairs={{16,0},{17,1},{18,2},{19,3},{20,4},{21,5},{22,6},{23,7},{24,8},{25... | collective-permute-start | bytes 1572872 | tf_op jit(solution)/shard_map/ppermute | solution.py:23
  325.2 32.6 %collective-permute-start.26 = (bf16[1,3,64,1152]{3,2,1,0:T(8,128)(2,1)S(1)}, bf16[1,3,64,1152]{3,2,1,0:T(8,128)(2,1)S(1)}, u32[]{:S(2)}, u32[]{:S(2)}) collective-permute-start(bf16[1,3,64,1152]{3,2,1,0:T(8,128)(2,1)S(1)} %fusion.327), channel_id=1, source_target_pairs={{0,2},{1,3},{2,0},{3,1},{4,6},{5,7},{6,4},{7,5},{8,10},{9,11},{10,... | collective-permute-start | bytes 1327112 | tf_op jit(solution)/shard_map/ppermute | solution.py:216
  327.7 30.1 %collective-permute-start.27 = (bf16[1,3,64,1152]{3,2,1,0:T(8,128)(2,1)S(1)}, bf16[1,3,64,1152]{3,2,1,0:T(8,128)(2,1)S(1)}, u32[]{:S(2)}, u32[]{:S(2)}) collective-permute-start(bf16[1,3,64,1152]{3,2,1,0:T(8,128)(2,1)S(1)} %fusion.327), channel_id=1, source_target_pairs={{0,3},{1,0},{2,1},{3,2},{4,7},{5,4},{6,5},{7,6},{8,11},{9,8},{10,9... | collective-permute-start | bytes 1327112 | tf_op jit(solution)/shard_map/ppermute | solution.py:216
  329.2 164.0 %collective-permute-start.24 = (f32[1,3,64,1024]{3,2,1,0:T(8,128)}, f32[1,3,64,1024]{3,2,1,0:T(8,128)}, u32[]{:S(2)}, u32[]{:S(2)}) collective-permute-start(f32[1,3,64,1024]{3,2,1,0:T(8,128)} %get-tuple-element.247), channel_id=1, source_target_pairs={{0,16},{1,17},{2,18},{3,19},{4,20},{5,21},{6,22},{7,23},{8,24},{9,... | collective-permute-start | bytes 2359304 | tf_op jit(solution)/shard_map/ppermute | solution.py:23
  379.7 23.0 %collective-permute-start.28 = (f32[1,8,64,128]{3,2,1,0:T(8,128)}, f32[1,8,64,128]{3,2,1,0:T(8,128)}, u32[]{:S(2)}, u32[]{:S(2)}) collective-permute-start(f32[1,8,64,128]{3,2,1,0:T(8,128)} %get-tuple-element.197), channel_id=1, source_target_pairs={{16,0},{17,1},{18,2},{19,3},{20,4},{21,5},{22,6},{23,7},{24,8},{25... | collective-permute-start | bytes 786440 | tf_op jit(solution)/shard_map/transpose(jvp())/ppermute | solution.py:23
  393.9 54.2 %collective-permute-start.53 = (bf16[256,512]{0,1:T(8,128)(2,1)}, bf16[256,512]{0,1:T(8,128)(2,1)}, u32[]{:S(2)}, u32[]{:S(2)}) collective-permute-start(bf16[256,512]{0,1:T(8,128)(2,1)} %convolution_convert_fusion.14), channel_id=1, source_target_pairs={{0,4},{4,8},{8,12},{12,0},{1,5},{5,9},{9,13},{13,1},{2,6},{6,10},{... | collective-permute-start | bytes 786440 | tf_op jit(solution)/shard_map/ppermute | solution.py:48
  396.2 53.2 %collective-permute-start.54 = (bf16[256,512]{0,1:T(8,128)(2,1)}, bf16[256,512]{0,1:T(8,128)(2,1)}, u32[]{:S(2)}, u32[]{:S(2)}) collective-permute-start(bf16[256,512]{0,1:T(8,128)(2,1)} %convolution_convert_fusion.13), channel_id=1, source_target_pairs={{0,8},{4,12},{8,0},{12,4},{1,9},{5,13},{9,1},{13,5},{2,10},{6,14},... | collective-permute-start | bytes 786440 | tf_op jit(solution)/shard_map/ppermute | solution.py:48
  402.7 46.7 %collective-permute-start.55 = (bf16[256,512]{0,1:T(8,128)(2,1)}, bf16[256,512]{0,1:T(8,128)(2,1)}, u32[]{:S(2)}, u32[]{:S(2)}) collective-permute-start(bf16[256,512]{0,1:T(8,128)(2,1)} %convolution_convert_fusion.12), channel_id=1, source_target_pairs={{0,12},{4,0},{8,4},{12,8},{1,13},{5,1},{9,5},{13,9},{2,14},{6,2},{... | collective-permute-start | bytes 786440 | tf_op jit(solution)/shard_map/ppermute | solution.py:48
  472.6 24.7 %collective-permute-start.30 = (bf16[1,3,64,1024]{3,2,1,0:T(8,128)(2,1)S(1)}, bf16[1,3,64,1024]{3,2,1,0:T(8,128)(2,1)S(1)}, u32[]{:S(2)}, u32[]{:S(2)}) collective-permute-start(bf16[1,3,64,1024]{3,2,1,0:T(8,128)(2,1)S(1)} %fusion.195), channel_id=1, source_target_pairs={{0,1},{1,2},{2,3},{3,0},{4,5},{5,6},{6,7},{7,4},{8,9},{9,10},{10,1... | collective-permute-start | bytes 1179656 | tf_op jit(solution)/shard_map/ppermute | solution.py:48
  484.4 21.4 %collective-permute-start.31 = (bf16[1,3,64,1024]{3,2,1,0:T(8,128)(2,1)S(1)}, bf16[1,3,64,1024]{3,2,1,0:T(8,128)(2,1)S(1)}, u32[]{:S(2)}, u32[]{:S(2)}) collective-permute-start(bf16[1,3,64,1024]{3,2,1,0:T(8,128)(2,1)S(1)} %fusion.192), channel_id=1, source_target_pairs={{0,2},{1,3},{2,0},{3,1},{4,6},{5,7},{6,4},{7,5},{8,10},{9,11},{10,... | collective-permute-start | bytes 1179656 | tf_op jit(solution)/shard_map/ppermute | solution.py:48
  485.4 20.4 %collective-permute-start.32 = (bf16[1,3,64,1024]{3,2,1,0:T(8,128)(2,1)S(1)}, bf16[1,3,64,1024]{3,2,1,0:T(8,128)(2,1)S(1)}, u32[]{:S(2)}, u32[]{:S(2)}) collective-permute-start(bf16[1,3,64,1024]{3,2,1,0:T(8,128)(2,1)S(1)} %fusion.189), channel_id=1, source_target_pairs={{0,3},{1,0},{2,1},{3,2},{4,7},{5,4},{6,5},{7,6},{8,11},{9,8},{10,9... | collective-permute-start | bytes 1179656 | tf_op jit(solution)/shard_map/ppermute | solution.py:48
  493.2 32.4 %collective-permute-start.50 = (bf16[256,1288]{0,1:T(8,128)(2,1)}, bf16[256,1288]{0,1:T(8,128)(2,1)}, u32[]{:S(2)}, u32[]{:S(2)}) collective-permute-start(bf16[256,1288]{0,1:T(8,128)(2,1)} %convolution_convert_fusion.2), channel_id=1, source_target_pairs={{0,4},{4,8},{8,12},{12,0},{1,5},{5,9},{9,13},{13,1},{2,6},{6,10},{... | collective-permute-start | bytes 1978376 | tf_op jit(solution)/shard_map/ppermute | solution.py:48
  493.2 32.7 %collective-permute-start.51 = (bf16[256,1288]{0,1:T(8,128)(2,1)}, bf16[256,1288]{0,1:T(8,128)(2,1)}, u32[]{:S(2)}, u32[]{:S(2)}) collective-permute-start(bf16[256,1288]{0,1:T(8,128)(2,1)} %convolution_convert_fusion.1), channel_id=1, source_target_pairs={{0,8},{4,12},{8,0},{12,4},{1,9},{5,13},{9,1},{13,5},{2,10},{6,14},... | collective-permute-start | bytes 1978376 | tf_op jit(solution)/shard_map/ppermute | solution.py:48
  497.3 28.7 %collective-permute-start.52 = (bf16[256,1288]{0,1:T(8,128)(2,1)}, bf16[256,1288]{0,1:T(8,128)(2,1)}, u32[]{:S(2)}, u32[]{:S(2)}) collective-permute-start(bf16[256,1288]{0,1:T(8,128)(2,1)} %convolution_convert_fusion), channel_id=1, source_target_pairs={{0,12},{4,0},{8,4},{12,8},{1,13},{5,1},{9,5},{13,9},{2,14},{6,2},{... | collective-permute-start | bytes 1978376 | tf_op jit(solution)/shard_map/ppermute | solution.py:48
  508.8 22.6 %collective-permute-start.33 = (bf16[1,3,64,1152]{3,2,1,0:T(8,128)(2,1)S(1)}, bf16[1,3,64,1152]{3,2,1,0:T(8,128)(2,1)S(1)}, u32[]{:S(2)}, u32[]{:S(2)}) collective-permute-start(bf16[1,3,64,1152]{3,2,1,0:T(8,128)(2,1)S(1)} %fusion.328), channel_id=1, source_target_pairs={{0,1},{1,2},{2,3},{3,0},{4,5},{5,6},{6,7},{7,4},{8,9},{9,10},{10,1... | collective-permute-start | bytes 1327112 | tf_op jit(solution)/shard_map/ppermute | solution.py:216
  517.8 29.7 %collective-permute-start.34 = (bf16[1,3,64,1152]{3,2,1,0:T(8,128)(2,1)S(1)}, bf16[1,3,64,1152]{3,2,1,0:T(8,128)(2,1)S(1)}, u32[]{:S(2)}, u32[]{:S(2)}) collective-permute-start(bf16[1,3,64,1152]{3,2,1,0:T(8,128)(2,1)S(1)} %fusion.328), channel_id=1, source_target_pairs={{0,2},{1,3},{2,0},{3,1},{4,6},{5,7},{6,4},{7,5},{8,10},{9,11},{10,... | collective-permute-start | bytes 1327112 | tf_op jit(solution)/shard_map/ppermute | solution.py:216
  525.6 21.9 %collective-permute-start.35 = (bf16[1,3,64,1152]{3,2,1,0:T(8,128)(2,1)S(1)}, bf16[1,3,64,1152]{3,2,1,0:T(8,128)(2,1)S(1)}, u32[]{:S(2)}, u32[]{:S(2)}) collective-permute-start(bf16[1,3,64,1152]{3,2,1,0:T(8,128)(2,1)S(1)} %fusion.328), channel_id=1, source_target_pairs={{0,3},{1,0},{2,1},{3,2},{4,7},{5,4},{6,5},{7,6},{8,11},{9,8},{10,9... | collective-permute-start | bytes 1327112 | tf_op jit(solution)/shard_map/ppermute | solution.py:216
  566.8 20.8 %collective-permute-start.36 = (f32[1,8,64,128]{3,2,1,0:T(8,128)}, f32[1,8,64,128]{3,2,1,0:T(8,128)}, u32[]{:S(2)}, u32[]{:S(2)}) collective-permute-start(f32[1,8,64,128]{3,2,1,0:T(8,128)} %get-tuple-element.179), channel_id=1, source_target_pairs={{16,0},{17,1},{18,2},{19,3},{20,4},{21,5},{22,6},{23,7},{24,8},{25... | collective-permute-start | bytes 786440 | tf_op jit(solution)/shard_map/transpose(jvp())/ppermute | solution.py:23
  578.6 53.5 %collective-permute-start.46 = (bf16[256,512]{0,1:T(8,128)(2,1)}, bf16[256,512]{0,1:T(8,128)(2,1)}, u32[]{:S(2)}, u32[]{:S(2)}) collective-permute-start(bf16[256,512]{0,1:T(8,128)(2,1)} %convolution_convert_fusion.17), channel_id=1, source_target_pairs={{0,4},{4,8},{8,12},{12,0},{1,5},{5,9},{9,13},{13,1},{2,6},{6,10},{... | collective-permute-start | bytes 786440 | tf_op jit(solution)/shard_map/ppermute | solution.py:48
  578.6 54.8 %collective-permute-start.47 = (bf16[256,512]{0,1:T(8,128)(2,1)}, bf16[256,512]{0,1:T(8,128)(2,1)}, u32[]{:S(2)}, u32[]{:S(2)}) collective-permute-start(bf16[256,512]{0,1:T(8,128)(2,1)} %convolution_convert_fusion.16), channel_id=1, source_target_pairs={{0,8},{4,12},{8,0},{12,4},{1,9},{5,13},{9,1},{13,5},{2,10},{6,14},... | collective-permute-start | bytes 786440 | tf_op jit(solution)/shard_map/ppermute | solution.py:48
  581.7 51.8 %collective-permute-start.48 = (bf16[256,512]{0,1:T(8,128)(2,1)}, bf16[256,512]{0,1:T(8,128)(2,1)}, u32[]{:S(2)}, u32[]{:S(2)}) collective-permute-start(bf16[256,512]{0,1:T(8,128)(2,1)} %convolution_convert_fusion.15), channel_id=1, source_target_pairs={{0,12},{4,0},{8,4},{12,8},{1,13},{5,1},{9,5},{13,9},{2,14},{6,2},{... | collective-permute-start | bytes 786440 | tf_op jit(solution)/shard_map/ppermute | solution.py:48
  615.1 63.7 %collective-permute-start.60 = (f32[5400]{0:T(1024)}, f32[5400]{0:T(1024)}, u32[]{:S(2)}, u32[]{:S(2)}) collective-permute-start(f32[5400]{0:T(1024)} %constant_dynamic-update-slice_fusion.5), channel_id=1, source_target_pairs={{0,4},{4,8},{8,12},{12,0},{1,5},{5,9},{9,13},{13,1},{2,6},{6,10},{... | collective-permute-start | bytes 64808 | tf_op jit(solution)/shard_map/ppermute | solution.py:36
  615.3 67.7 %collective-permute-start.61 = (f32[5400]{0:T(1024)}, f32[5400]{0:T(1024)}, u32[]{:S(2)}, u32[]{:S(2)}) collective-permute-start(f32[5400]{0:T(1024)} %constant_dynamic-update-slice_fusion.5), channel_id=1, source_target_pairs={{0,8},{4,12},{8,0},{12,4},{1,9},{5,13},{9,1},{13,5},{2,10},{6,14},... | collective-permute-start | bytes 64808 | tf_op jit(solution)/shard_map/ppermute | solution.py:36
  658.1 31.0 %collective-permute-start.38 = (bf16[1,3,64,1024]{3,2,1,0:T(8,128)(2,1)}, bf16[1,3,64,1024]{3,2,1,0:T(8,128)(2,1)}, u32[]{:S(2)}, u32[]{:S(2)}) collective-permute-start(bf16[1,3,64,1024]{3,2,1,0:T(8,128)(2,1)} %fusion.186), channel_id=1, source_target_pairs={{0,1},{1,2},{2,3},{3,0},{4,5},{5,6},{6,7},{7,4},{8,9},{9,10},{10,1... | collective-permute-start | bytes 1179656 | tf_op jit(solution)/shard_map/ppermute | solution.py:48
  671.4 24.5 %collective-permute-start.39 = (bf16[1,3,64,1024]{3,2,1,0:T(8,128)(2,1)}, bf16[1,3,64,1024]{3,2,1,0:T(8,128)(2,1)}, u32[]{:S(2)}, u32[]{:S(2)}) collective-permute-start(bf16[1,3,64,1024]{3,2,1,0:T(8,128)(2,1)} %fusion.183), channel_id=1, source_target_pairs={{0,2},{1,3},{2,0},{3,1},{4,6},{5,7},{6,4},{7,5},{8,10},{9,11},{10,... | collective-permute-start | bytes 1179656 | tf_op jit(solution)/shard_map/ppermute | solution.py:48
  676.0 20.8 %collective-permute-start.40 = (bf16[1,3,64,1024]{3,2,1,0:T(8,128)(2,1)}, bf16[1,3,64,1024]{3,2,1,0:T(8,128)(2,1)}, u32[]{:S(2)}, u32[]{:S(2)}) collective-permute-start(bf16[1,3,64,1024]{3,2,1,0:T(8,128)(2,1)} %fusion.180), channel_id=1, source_target_pairs={{0,3},{1,0},{2,1},{3,2},{4,7},{5,4},{6,5},{7,6},{8,11},{9,8},{10,9... | collective-permute-start | bytes 1179656 | tf_op jit(solution)/shard_map/ppermute | solution.py:48
  683.0 78.2 %collective-permute-start.42 = (f32[1,3,64,1024]{3,2,1,0:T(8,128)S(1)}, f32[1,3,64,1024]{3,2,1,0:T(8,128)}, u32[]{:S(2)}, u32[]{:S(2)}) collective-permute-start(f32[1,3,64,1024]{3,2,1,0:T(8,128)S(1)} %copy-done.22), channel_id=1, source_target_pairs={{0,16},{1,17},{2,18},{3,19},{4,20},{5,21},{6,22},{7,23},{8,24},{9,... | collective-permute-start | bytes 2359304 | tf_op jit(solution)/shard_map/ppermute | solution.py:23
  686.4 77.5 %collective-permute-start.56 = (bf16[256,1800]{0,1:T(8,128)(2,1)}, bf16[256,1800]{0,1:T(8,128)(2,1)}, u32[]{:S(2)}, u32[]{:S(2)}) collective-permute-start(bf16[256,1800]{0,1:T(8,128)(2,1)} %fusion.112), channel_id=1, source_target_pairs={{0,16},{1,17},{2,18},{3,19},{4,20},{5,21},{6,22},{7,23},{8,24},{9,... | collective-permute-start | bytes 2764808 | tf_op jit(solution)/shard_map/ppermute | solution.py:23
  696.7 23.7 %collective-permute-start.45 = (bf16[256,1288]{0,1:T(8,128)(2,1)}, bf16[256,1288]{0,1:T(8,128)(2,1)S(1)}, u32[]{:S(2)}, u32[]{:S(2)}) collective-permute-start(bf16[256,1288]{0,1:T(8,128)(2,1)} %convolution_convert_fusion.3), channel_id=1, source_target_pairs={{0,12},{4,0},{8,4},{12,8},{1,13},{5,1},{9,5},{13,9},{2,14},{6,2},{... | collective-permute-start | bytes 1978376 | tf_op jit(solution)/shard_map/ppermute | solution.py:48
  700.7 22.9 %collective-permute-start.57 = (f32[5400]{0:T(1024)S(1)}, f32[5400]{0:T(1024)S(1)}, u32[]{:S(2)}, u32[]{:S(2)}) collective-permute-start(f32[5400]{0:T(1024)S(1)} %constant_dynamic-update-slice_fusion.4), channel_id=1, source_target_pairs={{0,4},{4,8},{8,12},{12,0},{1,5},{5,9},{9,13},{13,1},{2,6},{6,10},{... | collective-permute-start | bytes 64808 | tf_op jit(solution)/shard_map/ppermute | solution.py:36
  723.7 40.2 %collective-permute-start.49 = (bf16[256,1800]{0,1:T(8,128)(2,1)}, bf16[256,1800]{0,1:T(8,128)(2,1)}, u32[]{:S(2)}, u32[]{:S(2)}) collective-permute-start(bf16[256,1800]{0,1:T(8,128)(2,1)} %fusion.113), channel_id=1, source_target_pairs={{16,0},{17,1},{18,2},{19,3},{20,4},{21,5},{22,6},{23,7},{24,8},{25... | collective-permute-start | bytes 2764808 | tf_op jit(solution)/shard_map/ppermute | solution.py:23
  727.6 33.5 %collective-permute-start.41 = (f32[1,2,64,1024]{3,2,1,0:T(8,128)}, f32[1,2,64,1024]{3,2,1,0:T(8,128)}, u32[]{:S(2)}, u32[]{:S(2)}) collective-permute-start(f32[1,2,64,1024]{3,2,1,0:T(8,128)} %slice.704), channel_id=1, source_target_pairs={{16,0},{17,1},{18,2},{19,3},{20,4},{21,5},{22,6},{23,7},{24,8},{25... | collective-permute-start | bytes 1572872 | tf_op jit(solution)/shard_map/ppermute | solution.py:23
  729.7 28.9 %collective-permute-start.63 = (f32[5400]{0:T(1024)S(1)}, f32[5400]{0:T(1024)S(1)}, u32[]{:S(2)}, u32[]{:S(2)}) collective-permute-start(f32[5400]{0:T(1024)S(1)} %broadcast_select_fusion.4), channel_id=1, source_target_pairs={{0,16},{16,0},{1,17},{17,1},{2,18},{18,2},{3,19},{19,3},{4,20},{20... | collective-permute-start | bytes 64808 | tf_op jit(solution)/shard_map/ppermute | solution.py:27
  766.7 20.4 %collective-permute-start.64 = (bf16[67840]{0:T(1024)(128)(2,1)}, bf16[67840]{0:T(1024)(128)(2,1)S(1)}, u32[]{:S(2)}, u32[]{:S(2)}) collective-permute-start(bf16[67840]{0:T(1024)(128)(2,1)} %pad_maximum_fusion.14), channel_id=1, source_target_pairs={{0,1},{1,2},{2,3},{3,0},{4,5},{5,6},{6,7},{7,4},{8,9},{9,10},{10,1... | collective-permute-start | bytes 407048 | tf_op jit(solution)/shard_map/ppermute | solution.py:36
  776.4 23.6 %collective-permute-start.66 = (bf16[67840]{0:T(1024)(128)(2,1)}, bf16[67840]{0:T(1024)(128)(2,1)}, u32[]{:S(2)}, u32[]{:S(2)}) collective-permute-start(bf16[67840]{0:T(1024)(128)(2,1)} %pad_maximum_fusion.14), channel_id=1, source_target_pairs={{0,3},{1,0},{2,1},{3,2},{4,7},{5,4},{6,5},{7,6},{8,11},{9,8},{10,9... | collective-permute-start | bytes 407048 | tf_op jit(solution)/shard_map/ppermute | solution.py:36
  (373 other events, 2964.2 us)
Sparse Core Ops, SparseCore 0:
  12.3 44.8 all-gather.4
  59.7 30.8 all-gather.6
